TPU v7x, 32 devices: a whole 2x2x4 slice. The times are simulated.
32 devices in a mesh: section: 4 (over z), seq: 8 (over y, x, core).
Axes of the slice: x: 2, y: 2, z: 4, core: 2. Of those that a mesh axis runs over, the one named last changes fastest.
Arguments:
- queries: bfloat16 [4, 1024, 8192], P('section', 'seq'), may hold values from -24 to 24
- keys: bfloat16 [4, 1024, 1024], P('section', 'seq'), may hold values from -24 to 24
- values: bfloat16 [4, 1024, 1024], P('section', 'seq'), may hold values from -6 to 6
- block_mask: int32 [4, 8, 8], P('section'), may hold values from 0 to 1, as said below
- block_live: int32 [4, 8], P('section'), may hold values from 1 to 128, as said below
Outputs:
- passed_context: bfloat16 [4, 1024, 8192], P('section', 'seq')
Inputs may be any that keep to these rules, and one draw needn't show every extreme that they name: block_mask[m, i, j] is 1 exactly when block j is block i or one of its ancestors in micro-batch m's tree: the first 4 blocks form a chain, each later block hangs below the chain's last block or a later block of lower index. `block_live`: the first 4 blocks of every micro-batch are full, its last block holds one live token.
All inputs are finite; a program needn't handle non-finite values.
Results may differ from a plain program's by a relative error of at most 0.0049.
Values may be sent and summed in bfloat16 or wider, within the bound.
No kernel may reach another device: no remote copies, remote signals or barrier semaphores. Data moves between devices by JAX's collectives and lax.ppermute only.
A program may use at most 128 MiB of HBM per device.

v0:
```python
import jax
import jax.numpy as jnp
from jax import lax
from jax.sharding import PartitionSpec as P

QUERY_HEADS = 64
KEY_VALUE_HEADS = 8
HEAD_SIZE = 128


def shifted(value, axis, by):
    count = lax.axis_size(axis)
    return lax.ppermute(value, axis, [(i, (i + by) % count) for i in range(count)])


def attend(qrows, qpos, keys_h, values_h, block_mask, block_live):
    total = keys_h.shape[0]
    nblk = block_mask.shape[0]
    width = total // nblk
    kpos = jnp.arange(total, dtype=jnp.int32)
    kblock = kpos // width
    key_live = kpos % width < jnp.repeat(block_live, width)
    qblock = qpos // width
    pick = (qblock[:, None] == jnp.arange(nblk, dtype=jnp.int32)[None, :]).astype(jnp.float32)
    allowed = jnp.repeat(jnp.dot(pick, block_mask.astype(jnp.float32)) > 0.5, width, axis=1)
    allowed = (
        allowed
        & key_live[None, :]
        & ((kblock[None, :] != qblock[:, None]) | (kpos[None, :] <= qpos[:, None]))
    )
    q_live = (qpos % width).astype(jnp.float32) < jnp.dot(pick, block_live.astype(jnp.float32))
    scale = qrows.shape[-1] ** (-0.5)
    scores = jnp.einsum("rgd,kd->grk", qrows, keys_h, preferred_element_type=jnp.float32) * scale
    scores = jnp.where(allowed[None], scores, -1e30)
    top = jnp.max(scores, axis=-1, keepdims=True)
    expo = jnp.where(allowed[None], jnp.exp(scores - top), 0.0)
    weights = (expo / jnp.sum(expo, axis=-1, keepdims=True)).astype(jnp.bfloat16)
    context = jnp.einsum("grk,kd->rgd", weights, values_h, preferred_element_type=jnp.float32)
    return jnp.where(q_live[:, None, None], context, 0.0).astype(jnp.bfloat16)


def per_device(queries, keys, values, block_mask, block_live):
    masks = block_mask[0]
    live = block_live[0]
    token_rows = queries.shape[1]
    nseq = lax.axis_size("seq")
    gathered_full = token_rows * nseq
    query_group_size = QUERY_HEADS // KEY_VALUE_HEADS
    gathered_keys, gathered_values = (
        lax.all_gather(keys, "seq", axis=1, tiled=True),
        lax.all_gather(values, "seq", axis=1, tiled=True),
    )
    query_head_rows = (
        queries[0]
        .reshape(token_rows, KEY_VALUE_HEADS, query_group_size, HEAD_SIZE)
        .transpose(1, 0, 2, 3)
    )
    key_head_rows = (
        gathered_keys[0].reshape(gathered_full, KEY_VALUE_HEADS, HEAD_SIZE).transpose(1, 0, 2)
    )
    value_head_rows = (
        gathered_values[0].reshape(gathered_full, KEY_VALUE_HEADS, HEAD_SIZE).transpose(1, 0, 2)
    )
    qpos = lax.axis_index("seq") * token_rows + jnp.arange(token_rows, dtype=jnp.int32)

    def head_fn(items):
        return attend(items[0], qpos, items[1], items[2], masks, live)

    out = lax.map(head_fn, (query_head_rows, key_head_rows, value_head_rows))
    local = out.transpose(1, 0, 2, 3).reshape(1, token_rows, QUERY_HEADS * HEAD_SIZE)
    return shifted(local, "section", 1)


def solution(mesh):
    placed = (
        P("section", "seq", None),
        P("section", "seq", None),
        P("section", "seq", None),
        P("section", None, None),
        P("section", None),
    )
    return jax.shard_map(
        per_device, mesh=mesh, in_specs=placed, out_specs=P("section", "seq", None), check_vma=False
    )
```

profile of v0, /device:TPU:0, one launch (start us, length us, event | category | flops | bytes accessed | tf_op | source)
XLA Modules:
  0.0 199.0 jit_solution(12889931288670990267)
XLA Ops:
  6.5 0.7 all-gather.3.cloned.1.call-update
  7.3 1.8 copy.11
  9.2 3.2 %copy.12 = bf16[1,128,8192]{1,2,0:T(8,128)(2,1)S(1)} copy(bf16[1,128,8192]{2,1,0:T(8,128)(2,1)} %param.7) | data formatting | bytes 4194304 | tf_op args[0]
  12.8 27.0 %all-gather.3.cloned.1.call-done = bf16[1,1024,1024]{2,1,0:T(8,128)(2,1)} async-done(((bf16[1,128,1024]{2,1,0:T(8,128)(2,1)}), bf16[1,1024,1024]{2,1,0:T(8,128)(2,1)}) %all-gather.3.cloned.1.call-update) | async-done | bytes 2097168 | tf_op jit(solution)/shard_map/all_gather | solution.py:51
  39.9 4.0 %copy.10 = bf16[1,1024,1024]{1,2,0:T(8,128)(2,1)} copy(bf16[1,1024,1024]{2,1,0:T(8,128)(2,1)} %all-gather.3.cloned.1.call-done) | data formatting | bytes 4194304 | tf_op jit(solution)/shard_map/all_gather | solution.py:51
  43.9 26.1 %all-gather.5.cloned.1.call-done = bf16[1,1024,1024]{1,2,0:T(8,128)(2,1)} async-done(((bf16[1,128,1024]{1,2,0:T(8,128)(2,1)}), bf16[1,1024,1024]{1,2,0:T(8,128)(2,1)}) %all-gather.5.cloned.1.call-update) | async-done | bytes 2097168 | tf_op jit(solution)/shard_map/all_gather | solution.py:50
  70.0 68.3 %while.18 = (s32[]{:T(128)}, bf16[8,128,8,128]{1,3,2,0:T(8,128)(2,1)}, f32[128]{0:T(128)S(1)}, bf16[8,1024,128]{1,2,0:T(8,128)(2,1)}, f32[128,8]{0,1:T(8,128)S(1...) while((s32[]{:T(128)}, ...), condition=%wide.region_3.4_spmd.clone.clone, body=%wide.region_0.3_spmd.clone.clone.sunk | while | flops 545149824 | bytes 9859981 | solution.py:69
  70.1 0.3 fusion.91
  70.4 4.6 %fusion.92 = (f32[8,128]{1,0:T(8,128)S(1)}, f32[8,128,1024]{1,2,0:T(8,128)}) fusion(pred[128,1024]{0,1:T(8,128)(4,1)S(1)} %fusion.91, bf16[8,128,8,128]{1,3,2,0:T(8,128)(2,1)S(1)} %get-tuple-element.474, s32[]{:T(128)} %get-tuple-element.457, bf16[8,1024,128]{1,2,0:T(8,128)(2,1)} %get-tuple-element.473), kind=kOutput, calls=%fused_computation.77.clone.1 | convolution fusion | flops 273679360 | bytes 4985856 | tf_op jit(solution)/shard_map/while/body/eval_jaxpr/sub | solution.py:36
  75.1 3.5 %fusion.94 = bf16[8,128,8,128]{1,3,2,0:T(8,128)(2,1)} fusion(bf16[8,128,8,128]{1,3,2,0:T(8,128)(2,1)} %get-tuple-element.458, s32[]{:T(128)} %get-tuple-element.457, f32[8,128,1024]{1,2,0:T(8,128)} %get-tuple-element.445, f32[8,128]{1,0:T(8,128)S(1)} %get-tuple-element.446, bf16[8,1024,128]{1,2,0:T(8,128)(2,1)} %get-tuple-element.470, ...), kind=kOutput, calls=%fused_computation.16.clone.1 | convolution fusion | flops 270794752 | bytes 4723840 | tf_op jit(solution)/shard_map/while/body/eval_jaxpr/grk,kd->rgd/dot_general | solution.py:38
  78.6 0.3 fusion.91
  79.0 4.6 %fusion.92 = (f32[8,128]{1,0:T(8,128)S(1)}, f32[8,128,1024]{1,2,0:T(8,128)}) fusion(pred[128,1024]{0,1:T(8,128)(4,1)S(1)} %fusion.91, bf16[8,128,8,128]{1,3,2,0:T(8,128)(2,1)S(1)} %get-tuple-element.474, s32[]{:T(128)} %get-tuple-element.457, bf16[8,1024,128]{1,2,0:T(8,128)(2,1)} %get-tuple-element.473), kind=kOutput, calls=%fused_computation.77.clone.1 | convolution fusion | flops 273679360 | bytes 4985856 | tf_op jit(solution)/shard_map/while/body/eval_jaxpr/sub | solution.py:36
  83.6 3.4 %fusion.94 = bf16[8,128,8,128]{1,3,2,0:T(8,128)(2,1)} fusion(bf16[8,128,8,128]{1,3,2,0:T(8,128)(2,1)} %get-tuple-element.458, s32[]{:T(128)} %get-tuple-element.457, f32[8,128,1024]{1,2,0:T(8,128)} %get-tuple-element.445, f32[8,128]{1,0:T(8,128)S(1)} %get-tuple-element.446, bf16[8,1024,128]{1,2,0:T(8,128)(2,1)} %get-tuple-element.470, ...), kind=kOutput, calls=%fused_computation.16.clone.1 | convolution fusion | flops 270794752 | bytes 4723840 | tf_op jit(solution)/shard_map/while/body/eval_jaxpr/grk,kd->rgd/dot_general | solution.py:38
  87.1 0.3 fusion.91
  87.5 4.6 %fusion.92 = (f32[8,128]{1,0:T(8,128)S(1)}, f32[8,128,1024]{1,2,0:T(8,128)}) fusion(pred[128,1024]{0,1:T(8,128)(4,1)S(1)} %fusion.91, bf16[8,128,8,128]{1,3,2,0:T(8,128)(2,1)S(1)} %get-tuple-element.474, s32[]{:T(128)} %get-tuple-element.457, bf16[8,1024,128]{1,2,0:T(8,128)(2,1)} %get-tuple-element.473), kind=kOutput, calls=%fused_computation.77.clone.1 | convolution fusion | flops 273679360 | bytes 4985856 | tf_op jit(solution)/shard_map/while/body/eval_jaxpr/sub | solution.py:36
  92.1 3.5 %fusion.94 = bf16[8,128,8,128]{1,3,2,0:T(8,128)(2,1)} fusion(bf16[8,128,8,128]{1,3,2,0:T(8,128)(2,1)} %get-tuple-element.458, s32[]{:T(128)} %get-tuple-element.457, f32[8,128,1024]{1,2,0:T(8,128)} %get-tuple-element.445, f32[8,128]{1,0:T(8,128)S(1)} %get-tuple-element.446, bf16[8,1024,128]{1,2,0:T(8,128)(2,1)} %get-tuple-element.470, ...), kind=kOutput, calls=%fused_computation.16.clone.1 | convolution fusion | flops 270794752 | bytes 4723840 | tf_op jit(solution)/shard_map/while/body/eval_jaxpr/grk,kd->rgd/dot_general | solution.py:38
  96.0 4.6 %fusion.92 = (f32[8,128]{1,0:T(8,128)S(1)}, f32[8,128,1024]{1,2,0:T(8,128)}) fusion(pred[128,1024]{0,1:T(8,128)(4,1)S(1)} %fusion.91, bf16[8,128,8,128]{1,3,2,0:T(8,128)(2,1)S(1)} %get-tuple-element.474, s32[]{:T(128)} %get-tuple-element.457, bf16[8,1024,128]{1,2,0:T(8,128)(2,1)} %get-tuple-element.473), kind=kOutput, calls=%fused_computation.77.clone.1 | convolution fusion | flops 273679360 | bytes 4985856 | tf_op jit(solution)/shard_map/while/body/eval_jaxpr/sub | solution.py:36
  100.7 3.4 %fusion.94 = bf16[8,128,8,128]{1,3,2,0:T(8,128)(2,1)} fusion(bf16[8,128,8,128]{1,3,2,0:T(8,128)(2,1)} %get-tuple-element.458, s32[]{:T(128)} %get-tuple-element.457, f32[8,128,1024]{1,2,0:T(8,128)} %get-tuple-element.445, f32[8,128]{1,0:T(8,128)S(1)} %get-tuple-element.446, bf16[8,1024,128]{1,2,0:T(8,128)(2,1)} %get-tuple-element.470, ...), kind=kOutput, calls=%fused_computation.16.clone.1 | convolution fusion | flops 270794752 | bytes 4723840 | tf_op jit(solution)/shard_map/while/body/eval_jaxpr/grk,kd->rgd/dot_general | solution.py:38
  104.6 4.6 %fusion.92 = (f32[8,128]{1,0:T(8,128)S(1)}, f32[8,128,1024]{1,2,0:T(8,128)}) fusion(pred[128,1024]{0,1:T(8,128)(4,1)S(1)} %fusion.91, bf16[8,128,8,128]{1,3,2,0:T(8,128)(2,1)S(1)} %get-tuple-element.474, s32[]{:T(128)} %get-tuple-element.457, bf16[8,1024,128]{1,2,0:T(8,128)(2,1)} %get-tuple-element.473), kind=kOutput, calls=%fused_computation.77.clone.1 | convolution fusion | flops 273679360 | bytes 4985856 | tf_op jit(solution)/shard_map/while/body/eval_jaxpr/sub | solution.py:36
  109.2 3.5 %fusion.94 = bf16[8,128,8,128]{1,3,2,0:T(8,128)(2,1)} fusion(bf16[8,128,8,128]{1,3,2,0:T(8,128)(2,1)} %get-tuple-element.458, s32[]{:T(128)} %get-tuple-element.457, f32[8,128,1024]{1,2,0:T(8,128)} %get-tuple-element.445, f32[8,128]{1,0:T(8,128)S(1)} %get-tuple-element.446, bf16[8,1024,128]{1,2,0:T(8,128)(2,1)} %get-tuple-element.470, ...), kind=kOutput, calls=%fused_computation.16.clone.1 | convolution fusion | flops 270794752 | bytes 4723840 | tf_op jit(solution)/shard_map/while/body/eval_jaxpr/grk,kd->rgd/dot_general | solution.py:38
  113.1 4.6 %fusion.92 = (f32[8,128]{1,0:T(8,128)S(1)}, f32[8,128,1024]{1,2,0:T(8,128)}) fusion(pred[128,1024]{0,1:T(8,128)(4,1)S(1)} %fusion.91, bf16[8,128,8,128]{1,3,2,0:T(8,128)(2,1)S(1)} %get-tuple-element.474, s32[]{:T(128)} %get-tuple-element.457, bf16[8,1024,128]{1,2,0:T(8,128)(2,1)} %get-tuple-element.473), kind=kOutput, calls=%fused_computation.77.clone.1 | convolution fusion | flops 273679360 | bytes 4985856 | tf_op jit(solution)/shard_map/while/body/eval_jaxpr/sub | solution.py:36
  117.7 3.4 %fusion.94 = bf16[8,128,8,128]{1,3,2,0:T(8,128)(2,1)} fusion(bf16[8,128,8,128]{1,3,2,0:T(8,128)(2,1)} %get-tuple-element.458, s32[]{:T(128)} %get-tuple-element.457, f32[8,128,1024]{1,2,0:T(8,128)} %get-tuple-element.445, f32[8,128]{1,0:T(8,128)S(1)} %get-tuple-element.446, bf16[8,1024,128]{1,2,0:T(8,128)(2,1)} %get-tuple-element.470, ...), kind=kOutput, calls=%fused_computation.16.clone.1 | convolution fusion | flops 270794752 | bytes 4723840 | tf_op jit(solution)/shard_map/while/body/eval_jaxpr/grk,kd->rgd/dot_general | solution.py:38
  121.3 0.3 fusion.91
  121.6 4.6 %fusion.92 = (f32[8,128]{1,0:T(8,128)S(1)}, f32[8,128,1024]{1,2,0:T(8,128)}) fusion(pred[128,1024]{0,1:T(8,128)(4,1)S(1)} %fusion.91, bf16[8,128,8,128]{1,3,2,0:T(8,128)(2,1)S(1)} %get-tuple-element.474, s32[]{:T(128)} %get-tuple-element.457, bf16[8,1024,128]{1,2,0:T(8,128)(2,1)} %get-tuple-element.473), kind=kOutput, calls=%fused_computation.77.clone.1 | convolution fusion | flops 273679360 | bytes 4985856 | tf_op jit(solution)/shard_map/while/body/eval_jaxpr/sub | solution.py:36
  126.3 3.5 %fusion.94 = bf16[8,128,8,128]{1,3,2,0:T(8,128)(2,1)} fusion(bf16[8,128,8,128]{1,3,2,0:T(8,128)(2,1)} %get-tuple-element.458, s32[]{:T(128)} %get-tuple-element.457, f32[8,128,1024]{1,2,0:T(8,128)} %get-tuple-element.445, f32[8,128]{1,0:T(8,128)S(1)} %get-tuple-element.446, bf16[8,1024,128]{1,2,0:T(8,128)(2,1)} %get-tuple-element.470, ...), kind=kOutput, calls=%fused_computation.16.clone.1 | convolution fusion | flops 270794752 | bytes 4723840 | tf_op jit(solution)/shard_map/while/body/eval_jaxpr/grk,kd->rgd/dot_general | solution.py:38
  129.8 0.3 fusion.91
  130.2 4.6 %fusion.92 = (f32[8,128]{1,0:T(8,128)S(1)}, f32[8,128,1024]{1,2,0:T(8,128)}) fusion(pred[128,1024]{0,1:T(8,128)(4,1)S(1)} %fusion.91, bf16[8,128,8,128]{1,3,2,0:T(8,128)(2,1)S(1)} %get-tuple-element.474, s32[]{:T(128)} %get-tuple-element.457, bf16[8,1024,128]{1,2,0:T(8,128)(2,1)} %get-tuple-element.473), kind=kOutput, calls=%fused_computation.77.clone.1 | convolution fusion | flops 273679360 | bytes 4985856 | tf_op jit(solution)/shard_map/while/body/eval_jaxpr/sub | solution.py:36
  134.8 3.4 %fusion.94 = bf16[8,128,8,128]{1,3,2,0:T(8,128)(2,1)} fusion(bf16[8,128,8,128]{1,3,2,0:T(8,128)(2,1)} %get-tuple-element.458, s32[]{:T(128)} %get-tuple-element.457, f32[8,128,1024]{1,2,0:T(8,128)} %get-tuple-element.445, f32[8,128]{1,0:T(8,128)S(1)} %get-tuple-element.446, bf16[8,1024,128]{1,2,0:T(8,128)(2,1)} %get-tuple-element.470, ...), kind=kOutput, calls=%fused_computation.16.clone.1 | convolution fusion | flops 270794752 | bytes 4723840 | tf_op jit(solution)/shard_map/while/body/eval_jaxpr/grk,kd->rgd/dot_general | solution.py:38
  138.3 2.9 %copy.17 = bf16[1,128,8192]{2,1,0:T(8,128)(2,1)S(1)} copy(bf16[1,128,8192]{1,2,0:T(8,128)(2,1)} %bitcast.107) | data formatting | bytes 4194304 | tf_op jit(solution)/shard_map/reshape | solution.py:70
  141.2 1.5 collective-permute-start
  142.7 48.1 %collective-permute-done = bf16[1,128,8192]{2,1,0:T(8,128)(2,1)S(1)} collective-permute-done((bf16[1,128,8192]{2,1,0:T(8,128)(2,1)S(1)}, bf16[1,128,8192]{2,1,0:T(8,128)(2,1)S(1)}, u32[]{:S(2)}, u32[]{:S(2)}) %collective-permute-start) | collective-permute-done | bytes 2097184 | tf_op jit(solution)/shard_map/ppermute | solution.py:13
  190.8 1.3 copy.30
  (54 shorter events, 2.4 us)
Async XLA Ops:
  6.5 33.3 %all-gather.3.cloned.1.call-start = ((), (), s32[]{:S(2)}) async-start(), calls=%async_computation | async-start | bytes 2359296 | tf_op jit(solution)/shard_map/all_gather | solution.py:51
  7.3 62.7 %all-gather.5.cloned.1.call-start = ((), (), s32[]{:S(2)}) async-start(), calls=%async_computation.1 | async-start | bytes 2359296 | tf_op jit(solution)/shard_map/all_gather | solution.py:50
  9.1 3.3 %copy-start.1 = (s32[1,8]{1,0:T(1,128)S(1)}, s32[1,8]{1,0:T(1,128)}, u32[]{:S(2)}) copy-start(s32[1,8]{1,0:T(1,128)} %param.11) | copy-start | bytes 100
  9.1 3.5 %copy-start = (s32[1,8,8]{2,1,0:T(8,128)S(1)}, s32[1,8,8]{2,1,0:T(8,128)}, u32[]{:S(2)}) copy-start(s32[1,8,8]{2,1,0:T(8,128)} %param.10) | copy-start | bytes 772
  141.2 49.6 %collective-permute-start = (bf16[1,128,8192]{2,1,0:T(8,128)(2,1)S(1)}, bf16[1,128,8192]{2,1,0:T(8,128)(2,1)S(1)}, u32[]{:S(2)}, u32[]{:S(2)}) collective-permute-start(bf16[1,128,8192]{2,1,0:T(8,128)(2,1)S(1)} %copy.17), channel_id=1, source_target_pairs={{0,8},{8,16},{16,24},{24,0},{1,9},{9,17},{17,25},{25,1},{2,10},{10... | collective-permute-start | bytes 6291464 | tf_op jit(solution)/shard_map/ppermute | solution.py:13
Sparse Core Ops, SparseCore 0:
  9.2 30.5 all-gather.2
  41.7 28.1 all-gather.4
where the time goes:
time: 200 us; the launch traced here: 199 us
  waiting for transfers between devices  102 us (51%)
  matrix products  65 us (32%)
  between operations  13.5 us (7%)
  local copies, waits for them, and re-layouts  13.2 us (7%)
  other arithmetic  3.59 us (2%)
    ppermute x1, waiting for transfers between devices, shifted(): lax.ppermute(value, axis, [(i, (i + by) % count) for i in range(count)])  48.1 us
    sub x8, matrix products, attend(): expo = jnp.where(allowed[None], jnp.exp(scores - top), 0.0)  37 us
    dot_general x8, matrix products, attend(): jnp.einsum('grk,kd->rgd', weights, values_h, preferred_element_type=jnp.f...  27.6 us
    all_gather x1, waiting for transfers between devices, per_device(): lax.all_gather(values, 'seq', axis=1, tiled=True)  27 us
    all_gather x1, waiting for transfers between devices, per_device(): lax.all_gather(keys, 'seq', axis=1, tiled=True)  26.1 us
    unnamed x7, local copies, waits for them, and re-layouts  6.34 us
  transfers between devices with their start and end apart: 3, of which 3 were waited for; matrix products, arithmetic and copies ran while one was open for 5% of the time, Pallas kernels for 0%

commit v1 on v0

v1 whole, which is shorter than its diff:
```python
import functools

import jax
import jax.numpy as jnp
from jax import lax
from jax.experimental import pallas as pl
from jax.experimental.pallas import tpu as pltpu
from jax.sharding import PartitionSpec as P

HEAD_SIZE = 128
NEG = -1e30
COST = pl.CostEstimate(flops=1, bytes_accessed=1, transcendentals=0)


def attend_kernel(scale, mask, live, q_ref, kv_ref, o_ref, bias, scores, peak, total):
    rows = q_ref.shape[0]
    group = q_ref.shape[1] // HEAD_SIZE
    blocks = [kv_ref.at[j] for j in range(kv_ref.shape[0])]
    width = blocks[0].shape[0]
    span = 2 * width
    me = lax.axis_index("seq")
    allowed = [mask[me, b] for b in range(len(blocks))]
    pairs = range(len(blocks) // 2)
    needed = [allowed[2 * t] + allowed[2 * t + 1] > 0 for t in pairs]

    @pl.when(pl.program_id(0) == 0)
    def _():
        row = lax.broadcasted_iota(jnp.int32, (rows, width), 0)
        col = lax.broadcasted_iota(jnp.int32, (rows, width), 1)
        for p in range(len(blocks)):
            limit = jnp.where(allowed[p] == 1, live[p], 0)
            reach = jnp.where(p == me, row, rows)
            bias[:, p * width : (p + 1) * width] = jnp.where(
                (col < limit) & (col <= reach), 0.0, NEG
            )

    peak[...] = jnp.full_like(peak, NEG)
    total[...] = jnp.zeros_like(total)
    for t in pairs:

        @pl.when(needed[t])
        def _():
            q = jnp.concatenate(
                [q_ref[:, g * HEAD_SIZE : (g + 1) * HEAD_SIZE] for g in range(group)], axis=0
            )
            keys = jnp.concatenate(
                [blocks[2 * t][:, :HEAD_SIZE], blocks[2 * t + 1][:, :HEAD_SIZE]], axis=0
            )
            part = lax.dot_general(
                q, keys, (((1,), (1,)), ((), ())), preferred_element_type=jnp.float32
            )
            part = part.reshape(group, rows, span) + bias[:, t * span : (t + 1) * span][None]
            part = part.reshape(group * rows, span)
            scores[:, t * span : (t + 1) * span] = part
            here = jnp.maximum(part[:, :width], part[:, width:])
            peak[...] = jnp.maximum(peak[...], here)

    top = jnp.max(peak[...], axis=1, keepdims=True)
    peak[...] = jnp.broadcast_to(top, peak.shape)
    for t in pairs:

        @pl.when(needed[t])
        def _():
            highest = jnp.concatenate([peak[...], peak[...]], axis=1)
            expo = jnp.exp2((scores[:, t * span : (t + 1) * span] - highest) * scale)
            vals = jnp.concatenate(
                [blocks[2 * t][:, HEAD_SIZE:], blocks[2 * t + 1][:, HEAD_SIZE:]], axis=0
            )
            both = jnp.concatenate([vals, jnp.ones((span, HEAD_SIZE), jnp.bfloat16)], axis=1)
            total[...] += jnp.dot(
                expo.astype(jnp.bfloat16), both, preferred_element_type=jnp.float32
            )

    alive = lax.broadcasted_iota(jnp.int32, (rows, HEAD_SIZE), 0) < live[me]
    for g in range(group):
        one = total[g * rows : (g + 1) * rows]
        out = jnp.where(alive, one[:, :HEAD_SIZE] / one[:, HEAD_SIZE:], 0.0)
        o_ref[:, g * HEAD_SIZE : (g + 1) * HEAD_SIZE] = out.astype(jnp.bfloat16)


def attend(mask, live, queries, first, heads, group, kv):
    rows = queries.shape[0]
    count, width = kv.shape[:2]
    step = group * HEAD_SIZE
    scale = HEAD_SIZE**-0.5 * 1.4426950408889634
    smem = pl.BlockSpec(memory_space=pltpu.SMEM)
    return pl.pallas_call(
        functools.partial(attend_kernel, scale),
        grid=(heads,),
        out_shape=jax.ShapeDtypeStruct((rows, heads * step), jnp.bfloat16),
        in_specs=[
            smem,
            smem,
            pl.BlockSpec((rows, step), lambda h: (0, first + h)),
            pl.BlockSpec((count, width, 2 * HEAD_SIZE), lambda h: (0, 0, h)),
        ],
        out_specs=pl.BlockSpec((rows, step), lambda h: (0, h)),
        scratch_shapes=[
            pltpu.VMEM((rows, count * width), jnp.float32),
            pltpu.VMEM((group * rows, count * width), jnp.float32),
            pltpu.VMEM((group * rows, width), jnp.float32),
            pltpu.VMEM((group * rows, 2 * HEAD_SIZE), jnp.float32),
        ],
        compiler_params=pltpu.CompilerParams(vmem_limit_bytes=40 * 2**20),
        cost_estimate=COST,
    )(mask, live, queries, kv)


def planar_kernel(scale, mask, live, q_ref, mine, theirs, o_ref):
    rows = q_ref.shape[0]
    group = q_ref.shape[1] // HEAD_SIZE
    chips, width = mine.shape[:2]
    me = lax.axis_index("seq")
    chip, core = me // 2, me % 2

    def body(n):
        slot = lax.broadcasted_iota(jnp.int32, (width, HEAD_SIZE), 0)
        zeroth = jnp.where(
            core == 0,
            mine[n - 1, :1, :HEAD_SIZE].astype(jnp.float32),
            theirs[n - 1, :1, :HEAD_SIZE].astype(jnp.float32),
        )
        zeroth = jnp.broadcast_to(zeroth, (width, HEAD_SIZE)).astype(jnp.bfloat16)
        keys, vals = [], []
        for j in range(n):
            r = (n - 1) ^ j
            for ref, block in ((mine, 2 * j + core), (theirs, 2 * j + 1 - core)):
                there = slot < jnp.where(mask[me, block] == 1, live[block], 0)
                if r == 0 and ref is mine:
                    keys.append(ref[r, :, :HEAD_SIZE])
                else:
                    keys.append(jnp.where(there, ref[r, :, :HEAD_SIZE], zeroth))
                vals.append(
                    jnp.concatenate(
                        [
                            jnp.where(there, ref[r, :, HEAD_SIZE:], jnp.bfloat16(0)),
                            jnp.where(there, jnp.bfloat16(1), jnp.bfloat16(0)),
                        ],
                        axis=1,
                    )
                )
        pairs = [jnp.concatenate(keys[2 * j : 2 * j + 2], axis=0) for j in range(n)]
        vals = jnp.concatenate(vals, axis=0)
        row = lax.broadcasted_iota(jnp.int32, (rows, width), 0)
        col = lax.broadcasted_iota(jnp.int32, (rows, width), 1)
        bias = jnp.where((col < live[me]) & (col <= row), 0.0, NEG)
        alive = lax.broadcasted_iota(jnp.int32, (rows, HEAD_SIZE), 0) < live[me]
        for g in range(group):
            cols = slice(g * HEAD_SIZE, (g + 1) * HEAD_SIZE)
            q = q_ref[:, cols]
            scores = []
            for j in range(n):
                part = lax.dot_general(
                    q, pairs[j], (((1,), (1,)), ((), ())), preferred_element_type=jnp.float32
                )
                own, other = part[:, :width], part[:, width:]
                scores += [own + bias if j == n - 1 else own, other]
            top = functools.reduce(jnp.maximum, scores)
            top = jnp.max(top, axis=1, keepdims=True)
            expo = [jnp.exp2((one - top) * scale).astype(jnp.bfloat16) for one in scores]
            out = jnp.dot(jnp.concatenate(expo, axis=1), vals, preferred_element_type=jnp.float32)
            out = jnp.where(alive, out[:, :HEAD_SIZE] / out[:, HEAD_SIZE:], 0.0)
            o_ref[:, cols] = out.astype(jnp.bfloat16)

    for n in range(1, chips + 1):
        pl.when(chip == n - 1)(functools.partial(body, n))


def attend_planar(mask, live, queries, first, heads, group, mine, theirs):
    rows = queries.shape[0]
    step = group * HEAD_SIZE
    smem = pl.BlockSpec(memory_space=pltpu.SMEM)
    kv = pl.BlockSpec(mine.shape[:2] + (2 * HEAD_SIZE,), lambda h: (0, 0, h))
    return pl.pallas_call(
        functools.partial(planar_kernel, HEAD_SIZE**-0.5 * 1.4426950408889634),
        grid=(heads,),
        out_shape=jax.ShapeDtypeStruct((rows, heads * step), jnp.bfloat16),
        in_specs=[smem, smem, pl.BlockSpec((rows, step), lambda h: (0, first + h)), kv, kv],
        out_specs=pl.BlockSpec((rows, step), lambda h: (0, h)),
        compiler_params=pltpu.CompilerParams(vmem_limit_bytes=40 * 2**20),
        cost_estimate=COST,
    )(mask, live, queries, mine, theirs)


def pack_kernel(mask, live, q_ref, k_ref, v_ref, sent, *o_refs):
    sent[:, : q_ref.shape[1]] = q_ref[...]
    sent[:, sent.shape[1] - HEAD_SIZE :] = jnp.zeros_like(sent[:, :HEAD_SIZE])
    blocks = live.shape[0]
    deep = 16
    row = lax.broadcasted_iota(jnp.int32, (deep, HEAD_SIZE), 0)
    col = lax.broadcasted_iota(jnp.int32, (deep, HEAD_SIZE), 1)
    tile = jnp.zeros((deep, HEAD_SIZE), jnp.int32)
    for j in range(blocks):
        tile = jnp.where((row == blocks) & (col == j), live[j], tile)
        for i in range(blocks):
            tile = jnp.where((row == i) & (col == j), mask[i, j], tile)
    sent[:deep, sent.shape[1] - HEAD_SIZE :] = tile.astype(jnp.float32).astype(sent.dtype)
    head = 0
    for n, ref in enumerate((sent,) + o_refs):
        begin = 0 if n else q_ref.shape[1]
        end = ref.shape[1] if n else ref.shape[1] - HEAD_SIZE
        for at in range(begin, end, 2 * HEAD_SIZE):
            cols = slice(head * HEAD_SIZE, (head + 1) * HEAD_SIZE)
            ref[:, at : at + HEAD_SIZE] = k_ref[:, cols]
            ref[:, at + HEAD_SIZE : at + 2 * HEAD_SIZE] = v_ref[:, cols]
            head += 1


def pack(mask, live, queries, keys, values, heads):
    rows, cols = keys.shape
    width = heads * 2 * HEAD_SIZE
    count = cols // (heads * HEAD_SIZE) - 1
    q_cols = heads * HEAD_SIZE * queries.shape[1] // cols
    smem = pl.BlockSpec(memory_space=pltpu.SMEM)

    def whole(shape):
        return pl.BlockSpec(shape, lambda i: (0, 0))

    shapes = [(rows, q_cols + width + HEAD_SIZE)] + [(rows, width)] * count
    return pl.pallas_call(
        pack_kernel,
        grid=(1,),
        out_shape=[jax.ShapeDtypeStruct(shape, keys.dtype) for shape in shapes],
        in_specs=[smem, smem, whole((rows, q_cols)), whole(keys.shape), whole(values.shape)],
        out_specs=[whole(shape) for shape in shapes],
        cost_estimate=COST,
    )(mask, live, queries, keys, values)


def pack_pairs(keys, values, heads):
    parts = []
    for h in heads:
        cols = slice(h * HEAD_SIZE, (h + 1) * HEAD_SIZE)
        parts += [keys[:, cols], values[:, cols]]
    return jnp.concatenate(parts, axis=1)


def after(value, *others):
    return lax.optimization_barrier((value,) + others)[0]


def on_plane(nsec, to):
    return [(s * 8 + i, s * 8 + to(i)) for s in range(nsec) for i in range(8)]


def exchange(part, nsec, by):
    return lax.ppermute(part, ("section", "seq"), on_plane(nsec, lambda i: i ^ by))


def per_device_8(queries, keys, values, block_mask, block_live):
    nsec = lax.axis_size("section")
    group = queries.shape[2] // keys.shape[2]
    step = group * HEAD_SIZE
    q, k, v = queries[0], keys[0], values[0]
    mask, live = block_mask[0], block_live[0]
    onward = [(i, (i + 1) % nsec) for i in range(nsec)]

    def on(value):
        return lax.ppermute(value, "section", onward)

    sent, *parts = pack(mask, live, q, k, v, 2)
    got = on(sent)

    def gather(part):
        return jnp.stack([part] + [exchange(part, nsec, by) for by in (2, 4, 6)])

    def both_cores(mine):
        return mine, exchange(mine, nsec, 1)

    def run(mask, live, q, first, kvs):
        return attend_planar(mask, live, q, first, 2, group, *kvs)

    mine1 = gather(parts[0])
    part2 = after(parts[1], mine1)
    ctx1 = run(mask, live, q, 2, both_cores(mine1))
    out1 = on(ctx1)
    mine2 = after(gather(part2), ctx1, got)
    part3 = after(parts[2], mine2)
    ctx2 = run(mask, live, q, 4, both_cores(mine2))
    out2 = on(ctx2)
    mine3 = after(gather(part3), ctx2, out1)
    part0 = after(got[:, 2 * step : -HEAD_SIZE], mine3)
    ctx3 = run(mask, live, q, 6, both_cores(mine3))
    out3 = on(ctx3)
    kvs0 = both_cores(after(gather(part0), ctx3, out2))
    blocks = live.shape[0]
    tab = got[: blocks + 1, -HEAD_SIZE:][:, :blocks].astype(jnp.int32)
    first = run(tab[:-1], tab[-1], got, 0, kvs0)
    return jnp.concatenate([first, out1, out2, out3], axis=1)[None]


def per_device(queries, keys, values, block_mask, block_live):
    nsec = lax.axis_size("section")
    group = queries.shape[2] // keys.shape[2]
    onward = [(i, (i + 1) % nsec) for i in range(nsec)]
    outs = []
    for h in range(0, keys.shape[2] // HEAD_SIZE, 2):
        kv = lax.all_gather(pack_pairs(keys[0], values[0], [h, h + 1]), "seq", axis=0)
        out = attend(block_mask[0], block_live[0], queries[0], h, 2, group, kv)
        outs.append(lax.ppermute(out, "section", onward))
    return jnp.concatenate(outs, axis=1)[None]


def solution(mesh):
    placed = (
        P("section", "seq", None),
        P("section", "seq", None),
        P("section", "seq", None),
        P("section", None, None),
        P("section", None),
    )
    body = per_device_8 if mesh.shape["seq"] == 8 else per_device
    return jax.shard_map(
        body, mesh=mesh, in_specs=placed, out_specs=P("section", "seq", None), check_vma=False
    )
```

time: 200 us -> 77.4 us (0.39)
  matrix products: 65 us -> 0 us
  waiting for transfers between devices: 102 us -> 41.6 us
  starting transfers between devices: 1.58 us -> 21 us
  between operations: 13.5 us -> 0.17 us
  local copies, waits for them, and re-layouts: 13.2 us -> 0.03 us
  Pallas kernels: 0 us -> 10.9 us
    all_gather x2 -> x0, waiting for transfers between devices: 53.2 us -> none  [the longest x1 27 us: per_device(): lax.all_gather(values, 'seq', axis=1, tiled=True)]
    sub x8 -> x0, matrix products: 37 us -> none  [attend(): expo = jnp.where(allowed[None], jnp.exp(scores - top), 0.0)]
    dot_general x10 -> x0, matrix products: 28 us -> none  [the longest x8 27.6 us: attend(): jnp.einsum('grk,kd->rgd', weights, values_h, preferred_element_type=jnp.f...]
    ppermute x1 -> x20, starting transfers between devices: 1.54 us -> 21 us  [the longest x16 17 us: exchange(): lax.ppermute(part, ('section', 'seq'), on_plane(nsec, lambda i: i ^ by))]
    pallas_call x0 -> x5, Pallas kernels: none -> 10.9 us  [the longest x4 8.5 us: attend_planar(): pl.pallas_call(functools.partial(planar_kernel, HEAD_SIZE ** (-0.5) * 1.4...]
    ppermute x1 -> x20, waiting for transfers between devices: 48.1 us -> 41.6 us  [the longest x16 25.3 us: exchange(): lax.ppermute(part, ('section', 'seq'), on_plane(nsec, lambda i: i ^ by))]
    unnamed x7 -> x8, local copies, waits for them, and re-layouts: 6.34 us -> 0.02 us
    all_gather x1 -> x0, local copies, waits for them, and re-layouts: 3.98 us -> none  [per_device(): lax.all_gather(values, 'seq', axis=1, tiled=True)]
  transfers between devices with their start and end apart: 3 -> 20, of which waited for: 3 -> 15; matrix products, arithmetic and copies ran while one was open for 5% -> 3% of each run, Pallas kernels for 0% -> 11%
where the time goes in v1:
time: 77.4 us; the launch traced here: 77.2 us
  waiting for transfers between devices  41.6 us (54%)
  starting transfers between devices  21 us (27%)
  Pallas kernels  10.9 us (14%)
  other arithmetic  3.54 us (5%)
    ppermute x16, waiting for transfers between devices, exchange(): lax.ppermute(part, ('section', 'seq'), on_plane(nsec, lambda i: i ^ by))  25.3 us
    ppermute x16, starting transfers between devices, exchange(): lax.ppermute(part, ('section', 'seq'), on_plane(nsec, lambda i: i ^ by))  17 us
    ppermute x4, waiting for transfers between devices, on(): return lax.ppermute(value, 'section', onward)  16.3 us
    pallas_call x4, Pallas kernels, attend_planar(): pl.pallas_call(functools.partial(planar_kernel, HEAD_SIZE ** (-0.5) * 1.4...  8.5 us
    ppermute x4, starting transfers between devices, on(): return lax.ppermute(value, 'section', onward)  4.01 us
    pallas_call x1, Pallas kernels, pack(): pl.pallas_call(pack_kernel, grid=(1,), out_shape=[jax.ShapeDtypeStruct(sh...  2.45 us
    another operation x4, other arithmetic, gather(): return jnp.stack([part] + [exchange(part, nsec, by) for by in (2, 4, 6)])  2.08 us
  transfers between devices with their start and end apart: 20, of which 15 were waited for; matrix products, arithmetic and copies ran while one was open for 3% of the time, Pallas kernels for 11%

profile of v1, /device:TPU:0, one launch (start us, length us, event | category | flops | bytes accessed | tf_op | source)
XLA Modules:
  0.0 77.2 jit_solution(4082959996724470408)
XLA Ops:
  0.0 2.4 %shard_map.55 = (bf16[128,2688]{1,0:T(8,128)(2,1)}, bf16[128,512]{1,0:T(8,128)(2,1)}, bf16[128,512]{1,0:T(8,128)(2,1)}, bf16[128,512]{1,0:T(8,128)(2,1)}) custom-call(s32[8,8]{1,0:T(8,128)} %bitcast.29, s32[8]{0:T(128)} %bitcast.33, bf16[128,8192]{1,0:T(8,128)(2,1)} %bitcast.25, bf16[128,1024]{1,0:T(8,128)(2,1)} %bitcast.38, bf16[128,1024]{1,0:T(8,128)(2,1)} %bitcast.39), custom_call_target="tpu_custom_call" | custom-call | flops 1 | bytes 1 | tf_op jit(solution)/shard_map/pallas_call | solution.py:220
  2.5 3.9 %collective-permute-start.3 = (bf16[128,512]{1,0:T(8,128)(2,1)}, bf16[128,512]{1,0:T(8,128)(2,1)S(1)}, u32[]{:S(2)}, u32[]{:S(2)}) collective-permute-start(bf16[128,512]{1,0:T(8,128)(2,1)} %get-tuple-element.18), channel_id=1, source_target_pairs={{0,6},{1,7},{2,4},{3,5},{4,2},{5,3},{6,0},{7,1},{8,14},{9,15},{10,... | collective-permute-start | bytes 393224 | tf_op jit(solution)/shard_map/ppermute | solution.py:247
  6.4 0.5 collective-permute-start.2
  7.0 2.0 %collective-permute-start = (bf16[128,2688]{1,0:T(8,128)(2,1)}, bf16[128,2688]{1,0:T(8,128)(2,1)S(1)}, u32[]{:S(2)}, u32[]{:S(2)}) collective-permute-start(bf16[128,2688]{1,0:T(8,128)(2,1)} %get-tuple-element.15), channel_id=1, source_target_pairs={{0,8},{8,16},{16,24},{24,0},{1,9},{9,17},{17,25},{25,1},{2,10},{10... | collective-permute-start | bytes 2064392 | tf_op jit(solution)/shard_map/ppermute | solution.py:259
  9.0 1.6 %collective-permute-done.3 = bf16[128,512]{1,0:T(8,128)(2,1)S(1)} collective-permute-done((bf16[128,512]{1,0:T(8,128)(2,1)}, bf16[128,512]{1,0:T(8,128)(2,1)S(1)}, u32[]{:S(2)}, u32[]{:S(2)}) %collective-permute-start.3) | collective-permute-done | bytes 131104 | tf_op jit(solution)/shard_map/ppermute | solution.py:247
  10.6 2.3 %collective-permute-done.2 = bf16[128,512]{1,0:T(8,128)(2,1)S(1)} collective-permute-done((bf16[128,512]{1,0:T(8,128)(2,1)}, bf16[128,512]{1,0:T(8,128)(2,1)S(1)}, u32[]{:S(2)}, u32[]{:S(2)}) %collective-permute-start.2) | collective-permute-done | bytes 131104 | tf_op jit(solution)/shard_map/ppermute | solution.py:247
  13.1 1.0 %pad_maximum_fusion.mine = bf16[4,128,512]{2,1,0:T(8,128)(2,1)S(1)} fusion(bf16[1,128,512]{2,1,0:T(8,128)(2,1)S(1)} %bitcast.43, bf16[1,128,512]{2,1,0:T(8,128)(2,1)S(1)} %bitcast.44, bf16[1,128,512]{2,1,0:T(8,128)(2,1)S(1)} %bitcast.48, bf16[1,128,512]{2,1,0:T(8,128)(2,1)} %bitcast.42), kind=kLoop, calls=%fused_computation.1 | loop fusion | flops 786432 | bytes 1048576 | tf_op jit(solution)/shard_map/stack | solution.py:265
  14.2 1.6 %collective-permute-start.6 = (bf16[128,512]{1,0:T(8,128)(2,1)}, bf16[128,512]{1,0:T(8,128)(2,1)S(1)}, u32[]{:S(2)}, u32[]{:S(2)}) collective-permute-start(bf16[128,512]{1,0:T(8,128)(2,1)} %get-tuple-element.19), channel_id=1, source_target_pairs={{0,6},{1,7},{2,4},{3,5},{4,2},{5,3},{6,0},{7,1},{8,14},{9,15},{10,... | collective-permute-start | bytes 393224 | tf_op jit(solution)/shard_map/ppermute | solution.py:247
  15.8 1.4 %collective-permute-start.5 = (bf16[128,512]{1,0:T(8,128)(2,1)}, bf16[128,512]{1,0:T(8,128)(2,1)S(1)}, u32[]{:S(2)}, u32[]{:S(2)}) collective-permute-start(bf16[128,512]{1,0:T(8,128)(2,1)} %get-tuple-element.19), channel_id=1, source_target_pairs={{0,4},{1,5},{2,6},{3,7},{4,0},{5,1},{6,2},{7,3},{8,12},{9,13},{10,... | collective-permute-start | bytes 393224 | tf_op jit(solution)/shard_map/ppermute | solution.py:247
  17.7 4.0 %collective-permute-done.6 = bf16[128,512]{1,0:T(8,128)(2,1)S(1)} collective-permute-done((bf16[128,512]{1,0:T(8,128)(2,1)}, bf16[128,512]{1,0:T(8,128)(2,1)S(1)}, u32[]{:S(2)}, u32[]{:S(2)}) %collective-permute-start.6) | collective-permute-done | bytes 131104 | tf_op jit(solution)/shard_map/ppermute | solution.py:247
  21.7 2.3 %collective-permute-done.5 = bf16[128,512]{1,0:T(8,128)(2,1)S(1)} collective-permute-done((bf16[128,512]{1,0:T(8,128)(2,1)}, bf16[128,512]{1,0:T(8,128)(2,1)S(1)}, u32[]{:S(2)}, u32[]{:S(2)}) %collective-permute-start.5) | collective-permute-done | bytes 131104 | tf_op jit(solution)/shard_map/ppermute | solution.py:247
  24.1 1.0 %pad_maximum_fusion.1.mine = bf16[4,128,512]{2,1,0:T(8,128)(2,1)S(1)} fusion(bf16[1,128,512]{2,1,0:T(8,128)(2,1)S(1)} %bitcast.45, bf16[1,128,512]{2,1,0:T(8,128)(2,1)S(1)} %bitcast.49, bf16[1,128,512]{2,1,0:T(8,128)(2,1)S(1)} %bitcast.52, bf16[1,128,512]{2,1,0:T(8,128)(2,1)} %bitcast.41), kind=kLoop, calls=%fused_computation.2 | loop fusion | flops 786432 | bytes 1048576 | tf_op jit(solution)/shard_map/stack | solution.py:265
  25.1 2.1 %shard_map.56 = bf16[128,2048]{1,0:T(8,128)(2,1)S(1)} custom-call(s32[8,8]{1,0:T(8,128)S(1)} %bitcast.30, s32[8]{0:T(128)S(1)} %bitcast.34, bf16[128,8192]{1,0:T(8,128)(2,1)S(1)} %bitcast.26, bf16[4,128,512]{2,1,0:T(8,128)(2,1)S(1)} %pad_maximum_fusion.mine, bf16[4,128,512]{2,1,0:T(8,128)(2,1)S(1)} %collective-permute-done.7.theirs), custom_call_target="tpu_custom_call" | custom-call | flops 1 | bytes 1 | tf_op jit(solution)/shard_map/pallas_call | solution.py:174
  27.3 1.6 %collective-permute-start.12 = (bf16[128,2048]{1,0:T(8,128)(2,1)S(1)}, bf16[128,2048]{1,0:T(8,128)(2,1)S(1)}, u32[]{:S(2)}, u32[]{:S(2)}) collective-permute-start(bf16[128,2048]{1,0:T(8,128)(2,1)S(1)} %shard_map.56), channel_id=1, source_target_pairs={{0,8},{8,16},{16,24},{24,0},{1,9},{9,17},{17,25},{25,1},{2,10},{10... | collective-permute-start | bytes 1572872 | tf_op jit(solution)/shard_map/ppermute | solution.py:259
  28.9 3.6 %collective-permute-start.10 = (bf16[128,512]{1,0:T(8,128)(2,1)S(1)}, bf16[128,512]{1,0:T(8,128)(2,1)S(1)}, u32[]{:S(2)}, u32[]{:S(2)}) collective-permute-start(bf16[128,512]{1,0:T(8,128)(2,1)S(1)} %copy-done.3), channel_id=1, source_target_pairs={{0,6},{1,7},{2,4},{3,5},{4,2},{5,3},{6,0},{7,1},{8,14},{9,15},{10,... | collective-permute-start | bytes 393224 | tf_op jit(solution)/shard_map/ppermute | solution.py:247
  32.6 0.8 %collective-permute-start.8 = (bf16[128,512]{1,0:T(8,128)(2,1)S(1)}, bf16[128,512]{1,0:T(8,128)(2,1)S(1)}, u32[]{:S(2)}, u32[]{:S(2)}) collective-permute-start(bf16[128,512]{1,0:T(8,128)(2,1)S(1)} %copy-done.3), channel_id=1, source_target_pairs={{0,2},{1,3},{2,0},{3,1},{4,6},{5,7},{6,4},{7,5},{8,10},{9,11},{10,... | collective-permute-start | bytes 393224 | tf_op jit(solution)/shard_map/ppermute | solution.py:247
  33.4 3.1 %collective-permute-done.10 = bf16[128,512]{1,0:T(8,128)(2,1)S(1)} collective-permute-done((bf16[128,512]{1,0:T(8,128)(2,1)S(1)}, bf16[128,512]{1,0:T(8,128)(2,1)S(1)}, u32[]{:S(2)}, u32[]{:S(2)}) %collective-permute-start.10) | collective-permute-done | bytes 131104 | tf_op jit(solution)/shard_map/ppermute | solution.py:247
  36.5 2.7 %collective-permute-done.9 = bf16[128,512]{1,0:T(8,128)(2,1)S(1)} collective-permute-done((bf16[128,512]{1,0:T(8,128)(2,1)S(1)}, bf16[128,512]{1,0:T(8,128)(2,1)S(1)}, u32[]{:S(2)}, u32[]{:S(2)}) %collective-permute-start.9) | collective-permute-done | bytes 131104 | tf_op jit(solution)/shard_map/ppermute | solution.py:247
  39.2 0.6 collective-permute-done.8
  39.8 2.1 %shard_map.57 = bf16[128,2048]{1,0:T(8,128)(2,1)S(1)} custom-call(s32[8,8]{1,0:T(8,128)S(1)} %bitcast.31, s32[8]{0:T(128)S(1)} %bitcast.35, bf16[128,8192]{1,0:T(8,128)(2,1)S(1)} %bitcast.27, bf16[4,128,512]{2,1,0:T(8,128)(2,1)S(1)} %pad_maximum_fusion.1.mine, bf16[4,128,512]{2,1,0:T(8,128)(2,1)S(1)} %collective-permute-done.11.theirs), custom_call_target="tpu_custom_call" | custom-call | flops 1 | bytes 1 | tf_op jit(solution)/shard_map/pallas_call | solution.py:174
  42.0 1.5 %collective-permute-done.12 = bf16[128,2048]{1,0:T(8,128)(2,1)S(1)} collective-permute-done((bf16[128,2048]{1,0:T(8,128)(2,1)S(1)}, bf16[128,2048]{1,0:T(8,128)(2,1)S(1)}, u32[]{:S(2)}, u32[]{:S(2)}) %collective-permute-start.12) | collective-permute-done | bytes 524320 | tf_op jit(solution)/shard_map/ppermute | solution.py:259
  43.9 3.5 %collective-permute-start.15 = (bf16[128,512]{1,0:T(8,128)(2,1)S(1)}, bf16[128,512]{1,0:T(8,128)(2,1)S(1)}, u32[]{:S(2)}, u32[]{:S(2)}) collective-permute-start(bf16[128,512]{1,0:T(8,128)(2,1)S(1)} %slice.21), channel_id=1, source_target_pairs={{0,6},{1,7},{2,4},{3,5},{4,2},{5,3},{6,0},{7,1},{8,14},{9,15},{10,... | collective-permute-start | bytes 393224 | tf_op jit(solution)/shard_map/ppermute | solution.py:247
  47.4 0.8 %collective-permute-start.13 = (bf16[128,512]{1,0:T(8,128)(2,1)S(1)}, bf16[128,512]{1,0:T(8,128)(2,1)S(1)}, u32[]{:S(2)}, u32[]{:S(2)}) collective-permute-start(bf16[128,512]{1,0:T(8,128)(2,1)S(1)} %slice.21), channel_id=1, source_target_pairs={{0,2},{1,3},{2,0},{3,1},{4,6},{5,7},{6,4},{7,5},{8,10},{9,11},{10,... | collective-permute-start | bytes 393224 | tf_op jit(solution)/shard_map/ppermute | solution.py:247
  48.2 3.3 %collective-permute-done.15 = bf16[128,512]{1,0:T(8,128)(2,1)S(1)} collective-permute-done((bf16[128,512]{1,0:T(8,128)(2,1)S(1)}, bf16[128,512]{1,0:T(8,128)(2,1)S(1)}, u32[]{:S(2)}, u32[]{:S(2)}) %collective-permute-start.15) | collective-permute-done | bytes 131104 | tf_op jit(solution)/shard_map/ppermute | solution.py:247
  51.5 2.7 %collective-permute-done.14 = bf16[128,512]{1,0:T(8,128)(2,1)S(1)} collective-permute-done((bf16[128,512]{1,0:T(8,128)(2,1)S(1)}, bf16[128,512]{1,0:T(8,128)(2,1)S(1)}, u32[]{:S(2)}, u32[]{:S(2)}) %collective-permute-start.14) | collective-permute-done | bytes 131104 | tf_op jit(solution)/shard_map/ppermute | solution.py:247
  54.2 0.6 collective-permute-done.13
  54.8 2.1 %shard_map.58 = bf16[128,2048]{1,0:T(8,128)(2,1)S(1)} custom-call(s32[8,8]{1,0:T(8,128)S(1)} %bitcast.32, s32[8]{0:T(128)S(1)} %bitcast.36, bf16[128,8192]{1,0:T(8,128)(2,1)S(1)} %bitcast.28, bf16[4,128,512]{2,1,0:T(8,128)(2,1)S(1)} %pad_maximum_fusion.2.mine, bf16[4,128,512]{2,1,0:T(8,128)(2,1)S(1)} %collective-permute-done.16.theirs), custom_call_target="tpu_custom_call" | custom-call | flops 1 | bytes 1 | tf_op jit(solution)/shard_map/pallas_call | solution.py:174
  57.0 2.7 %collective-permute-done.17 = bf16[128,2048]{1,0:T(8,128)(2,1)S(1)} collective-permute-done((bf16[128,2048]{1,0:T(8,128)(2,1)S(1)}, bf16[128,2048]{1,0:T(8,128)(2,1)S(1)}, u32[]{:S(2)}, u32[]{:S(2)}) %collective-permute-start.17) | collective-permute-done | bytes 524320 | tf_op jit(solution)/shard_map/ppermute | solution.py:259
  59.7 1.9 %collective-permute-done.18.theirs = bf16[4,128,512]{2,1,0:T(8,128)(2,1)S(1)} collective-permute-done((bf16[4,128,512]{2,1,0:T(8,128)(2,1)S(1)}, bf16[4,128,512]{2,1,0:T(8,128)(2,1)S(1)}, u32[]{:S(2)}, u32[]{:S(2)}) %collective-permute-start.18) | collective-permute-done | bytes 524320 | tf_op jit(solution)/shard_map/ppermute | solution.py:247
  61.5 2.1 %shard_map.59 = bf16[128,2048]{1,0:T(8,128)(2,1)S(1)} custom-call(s32[8,8]{1,0:T(8,128)S(1)} %slice.19.mask, s32[8]{0:T(128)S(1)} %slice_bitcast_fusion.live, bf16[128,2688]{1,0:T(8,128)(2,1)S(1)} %collective-permute-done.q_ref, bf16[4,128,512]{2,1,0:T(8,128)(2,1)S(1)} %pad_maximum_fusion.3.mine, bf16[4,128,512]{2,1,0:T(8,128)(2,1)S(1)} %collective-permute-done.18.theirs), custom_call_target="tpu_custom_call" | custom-call | flops 1 | bytes 1 | tf_op jit(solution)/shard_map/pallas_call | solution.py:174
  63.7 12.1 %collective-permute-done.19 = bf16[128,2048]{1,0:T(8,128)(2,1)S(1)} collective-permute-done((bf16[128,2048]{1,0:T(8,128)(2,1)S(1)}, bf16[128,2048]{1,0:T(8,128)(2,1)S(1)}, u32[]{:S(2)}, u32[]{:S(2)}) %collective-permute-start.19) | collective-permute-done | bytes 524320 | tf_op jit(solution)/shard_map/ppermute | solution.py:259
  75.8 1.5 %maximum_bitcast_fusion = bf16[1,128,8192]{2,1,0:T(8,128)(2,1)} fusion(bf16[128,2048]{1,0:T(8,128)(2,1)S(1)} %collective-permute-done.19, bf16[128,2048]{1,0:T(8,128)(2,1)S(1)} %collective-permute-done.17, bf16[128,2048]{1,0:T(8,128)(2,1)S(1)} %collective-permute-done.12, bf16[128,2048]{1,0:T(8,128)(2,1)S(1)} %shard_map.59), kind=kLoop, calls=%fused_computation | loop fusion | flops 8388608 | bytes 4194304 | tf_op jit(solution)/shard_map/broadcast_in_dim | solution.py:289
  (30 shorter events, 1.6 us)
Async XLA Ops:
  0.0 25.1 %copy-start = (bf16[1,128,8192]{2,1,0:T(8,128)(2,1)S(1)}, bf16[1,128,8192]{2,1,0:T(8,128)(2,1)}, u32[]{:S(2)}) copy-start(bf16[1,128,8192]{2,1,0:T(8,128)(2,1)} %param.5) | copy-start | bytes 6291460
  0.0 25.1 %copy-start.1 = (s32[1,8,8]{2,1,0:T(8,128)S(1)}, s32[1,8,8]{2,1,0:T(8,128)}, u32[]{:S(2)}) copy-start(s32[1,8,8]{2,1,0:T(8,128)} %param.8) | copy-start | bytes 772
  0.0 25.1 %copy-start.2 = (s32[1,8]{1,0:T(1,128)S(1)}, s32[1,8]{1,0:T(1,128)}, u32[]{:S(2)}) copy-start(s32[1,8]{1,0:T(1,128)} %param.9) | copy-start | bytes 100
  2.5 8.1 %collective-permute-start.3 = (bf16[128,512]{1,0:T(8,128)(2,1)}, bf16[128,512]{1,0:T(8,128)(2,1)S(1)}, u32[]{:S(2)}, u32[]{:S(2)}) collective-permute-start(bf16[128,512]{1,0:T(8,128)(2,1)} %get-tuple-element.18), channel_id=1, source_target_pairs={{0,6},{1,7},{2,4},{3,5},{4,2},{5,3},{6,0},{7,1},{8,14},{9,15},{10,... | collective-permute-start | bytes 393224 | tf_op jit(solution)/shard_map/ppermute | solution.py:247
  6.4 6.5 %collective-permute-start.2 = (bf16[128,512]{1,0:T(8,128)(2,1)}, bf16[128,512]{1,0:T(8,128)(2,1)S(1)}, u32[]{:S(2)}, u32[]{:S(2)}) collective-permute-start(bf16[128,512]{1,0:T(8,128)(2,1)} %get-tuple-element.18), channel_id=1, source_target_pairs={{0,4},{1,5},{2,6},{3,7},{4,0},{5,1},{6,2},{7,3},{8,12},{9,13},{10,... | collective-permute-start | bytes 393224 | tf_op jit(solution)/shard_map/ppermute | solution.py:247
  6.9 6.3 %collective-permute-start.1 = (bf16[128,512]{1,0:T(8,128)(2,1)}, bf16[128,512]{1,0:T(8,128)(2,1)S(1)}, u32[]{:S(2)}, u32[]{:S(2)}) collective-permute-start(bf16[128,512]{1,0:T(8,128)(2,1)} %get-tuple-element.18), channel_id=1, source_target_pairs={{0,2},{1,3},{2,0},{3,1},{4,6},{5,7},{6,4},{7,5},{8,10},{9,11},{10,... | collective-permute-start | bytes 393224 | tf_op jit(solution)/shard_map/ppermute | solution.py:247
  7.0 20.2 %collective-permute-start = (bf16[128,2688]{1,0:T(8,128)(2,1)}, bf16[128,2688]{1,0:T(8,128)(2,1)S(1)}, u32[]{:S(2)}, u32[]{:S(2)}) collective-permute-start(bf16[128,2688]{1,0:T(8,128)(2,1)} %get-tuple-element.15), channel_id=1, source_target_pairs={{0,8},{8,16},{16,24},{24,0},{1,9},{9,17},{17,25},{25,1},{2,10},{10... | collective-permute-start | bytes 2064392 | tf_op jit(solution)/shard_map/ppermute | solution.py:259
  14.1 10.9 %collective-permute-start.7 = (bf16[4,128,512]{2,1,0:T(8,128)(2,1)S(1)}, bf16[4,128,512]{2,1,0:T(8,128)(2,1)S(1)}, u32[]{:S(2)}, u32[]{:S(2)}) collective-permute-start(bf16[4,128,512]{2,1,0:T(8,128)(2,1)S(1)} %pad_maximum_fusion.mine), channel_id=1, source_target_pairs={{0,1},{1,0},{2,3},{3,2},{4,5},{5,4},{6,7},{7,6},{8,9},{9,8},{10,11... | collective-permute-start | bytes 1572872 | tf_op jit(solution)/shard_map/ppermute | solution.py:247
  14.2 7.5 %collective-permute-start.6 = (bf16[128,512]{1,0:T(8,128)(2,1)}, bf16[128,512]{1,0:T(8,128)(2,1)S(1)}, u32[]{:S(2)}, u32[]{:S(2)}) collective-permute-start(bf16[128,512]{1,0:T(8,128)(2,1)} %get-tuple-element.19), channel_id=1, source_target_pairs={{0,6},{1,7},{2,4},{3,5},{4,2},{5,3},{6,0},{7,1},{8,14},{9,15},{10,... | collective-permute-start | bytes 393224 | tf_op jit(solution)/shard_map/ppermute | solution.py:247
  15.8 8.2 %collective-permute-start.5 = (bf16[128,512]{1,0:T(8,128)(2,1)}, bf16[128,512]{1,0:T(8,128)(2,1)S(1)}, u32[]{:S(2)}, u32[]{:S(2)}) collective-permute-start(bf16[128,512]{1,0:T(8,128)(2,1)} %get-tuple-element.19), channel_id=1, source_target_pairs={{0,4},{1,5},{2,6},{3,7},{4,0},{5,1},{6,2},{7,3},{8,12},{9,13},{10,... | collective-permute-start | bytes 393224 | tf_op jit(solution)/shard_map/ppermute | solution.py:247
  17.2 6.8 %collective-permute-start.4 = (bf16[128,512]{1,0:T(8,128)(2,1)}, bf16[128,512]{1,0:T(8,128)(2,1)S(1)}, u32[]{:S(2)}, u32[]{:S(2)}) collective-permute-start(bf16[128,512]{1,0:T(8,128)(2,1)} %get-tuple-element.19), channel_id=1, source_target_pairs={{0,2},{1,3},{2,0},{3,1},{4,6},{5,7},{6,4},{7,5},{8,10},{9,11},{10,... | collective-permute-start | bytes 393224 | tf_op jit(solution)/shard_map/ppermute | solution.py:247
  25.0 3.9 %copy-start.3 = (bf16[128,512]{1,0:T(8,128)(2,1)S(1)}, bf16[128,512]{1,0:T(8,128)(2,1)}, u32[]{:S(2)}) copy-start(bf16[128,512]{1,0:T(8,128)(2,1)} %get-tuple-element.21) | copy-start | bytes 393220
  27.2 12.6 %collective-permute-start.11 = (bf16[4,128,512]{2,1,0:T(8,128)(2,1)S(1)}, bf16[4,128,512]{2,1,0:T(8,128)(2,1)S(1)}, u32[]{:S(2)}, u32[]{:S(2)}) collective-permute-start(bf16[4,128,512]{2,1,0:T(8,128)(2,1)S(1)} %pad_maximum_fusion.1.mine), channel_id=1, source_target_pairs={{0,1},{1,0},{2,3},{3,2},{4,5},{5,4},{6,7},{7,6},{8,9},{9,8},{10,11... | collective-permute-start | bytes 1572872 | tf_op jit(solution)/shard_map/ppermute | solution.py:247
  27.3 16.2 %collective-permute-start.12 = (bf16[128,2048]{1,0:T(8,128)(2,1)S(1)}, bf16[128,2048]{1,0:T(8,128)(2,1)S(1)}, u32[]{:S(2)}, u32[]{:S(2)}) collective-permute-start(bf16[128,2048]{1,0:T(8,128)(2,1)S(1)} %shard_map.56), channel_id=1, source_target_pairs={{0,8},{8,16},{16,24},{24,0},{1,9},{9,17},{17,25},{25,1},{2,10},{10... | collective-permute-start | bytes 1572872 | tf_op jit(solution)/shard_map/ppermute | solution.py:259
  28.9 7.6 %collective-permute-start.10 = (bf16[128,512]{1,0:T(8,128)(2,1)S(1)}, bf16[128,512]{1,0:T(8,128)(2,1)S(1)}, u32[]{:S(2)}, u32[]{:S(2)}) collective-permute-start(bf16[128,512]{1,0:T(8,128)(2,1)S(1)} %copy-done.3), channel_id=1, source_target_pairs={{0,6},{1,7},{2,4},{3,5},{4,2},{5,3},{6,0},{7,1},{8,14},{9,15},{10,... | collective-permute-start | bytes 393224 | tf_op jit(solution)/shard_map/ppermute | solution.py:247
  32.6 6.6 %collective-permute-start.9 = (bf16[128,512]{1,0:T(8,128)(2,1)S(1)}, bf16[128,512]{1,0:T(8,128)(2,1)S(1)}, u32[]{:S(2)}, u32[]{:S(2)}) collective-permute-start(bf16[128,512]{1,0:T(8,128)(2,1)S(1)} %copy-done.3), channel_id=1, source_target_pairs={{0,4},{1,5},{2,6},{3,7},{4,0},{5,1},{6,2},{7,3},{8,12},{9,13},{10,... | collective-permute-start | bytes 393224 | tf_op jit(solution)/shard_map/ppermute | solution.py:247
  32.6 7.2 %collective-permute-start.8 = (bf16[128,512]{1,0:T(8,128)(2,1)S(1)}, bf16[128,512]{1,0:T(8,128)(2,1)S(1)}, u32[]{:S(2)}, u32[]{:S(2)}) collective-permute-start(bf16[128,512]{1,0:T(8,128)(2,1)S(1)} %copy-done.3), channel_id=1, source_target_pairs={{0,2},{1,3},{2,0},{3,1},{4,6},{5,7},{6,4},{7,5},{8,10},{9,11},{10,... | collective-permute-start | bytes 393224 | tf_op jit(solution)/shard_map/ppermute | solution.py:247
  43.5 11.3 %collective-permute-start.16 = (bf16[4,128,512]{2,1,0:T(8,128)(2,1)S(1)}, bf16[4,128,512]{2,1,0:T(8,128)(2,1)S(1)}, u32[]{:S(2)}, u32[]{:S(2)}) collective-permute-start(bf16[4,128,512]{2,1,0:T(8,128)(2,1)S(1)} %pad_maximum_fusion.2.mine), channel_id=1, source_target_pairs={{0,1},{1,0},{2,3},{3,2},{4,5},{5,4},{6,7},{7,6},{8,9},{9,8},{10,11... | collective-permute-start | bytes 1572872 | tf_op jit(solution)/shard_map/ppermute | solution.py:247
  43.5 16.1 %collective-permute-start.17 = (bf16[128,2048]{1,0:T(8,128)(2,1)S(1)}, bf16[128,2048]{1,0:T(8,128)(2,1)S(1)}, u32[]{:S(2)}, u32[]{:S(2)}) collective-permute-start(bf16[128,2048]{1,0:T(8,128)(2,1)S(1)} %shard_map.57), channel_id=1, source_target_pairs={{0,8},{8,16},{16,24},{24,0},{1,9},{9,17},{17,25},{25,1},{2,10},{10... | collective-permute-start | bytes 1572872 | tf_op jit(solution)/shard_map/ppermute | solution.py:259
  43.9 7.6 %collective-permute-start.15 = (bf16[128,512]{1,0:T(8,128)(2,1)S(1)}, bf16[128,512]{1,0:T(8,128)(2,1)S(1)}, u32[]{:S(2)}, u32[]{:S(2)}) collective-permute-start(bf16[128,512]{1,0:T(8,128)(2,1)S(1)} %slice.21), channel_id=1, source_target_pairs={{0,6},{1,7},{2,4},{3,5},{4,2},{5,3},{6,0},{7,1},{8,14},{9,15},{10,... | collective-permute-start | bytes 393224 | tf_op jit(solution)/shard_map/ppermute | solution.py:247
  47.4 6.8 %collective-permute-start.14 = (bf16[128,512]{1,0:T(8,128)(2,1)S(1)}, bf16[128,512]{1,0:T(8,128)(2,1)S(1)}, u32[]{:S(2)}, u32[]{:S(2)}) collective-permute-start(bf16[128,512]{1,0:T(8,128)(2,1)S(1)} %slice.21), channel_id=1, source_target_pairs={{0,4},{1,5},{2,6},{3,7},{4,0},{5,1},{6,2},{7,3},{8,12},{9,13},{10,... | collective-permute-start | bytes 393224 | tf_op jit(solution)/shard_map/ppermute | solution.py:247
  47.4 7.4 %collective-permute-start.13 = (bf16[128,512]{1,0:T(8,128)(2,1)S(1)}, bf16[128,512]{1,0:T(8,128)(2,1)S(1)}, u32[]{:S(2)}, u32[]{:S(2)}) collective-permute-start(bf16[128,512]{1,0:T(8,128)(2,1)S(1)} %slice.21), channel_id=1, source_target_pairs={{0,2},{1,3},{2,0},{3,1},{4,6},{5,7},{6,4},{7,5},{8,10},{9,11},{10,... | collective-permute-start | bytes 393224 | tf_op jit(solution)/shard_map/ppermute | solution.py:247
  59.6 1.9 %collective-permute-start.18 = (bf16[4,128,512]{2,1,0:T(8,128)(2,1)S(1)}, bf16[4,128,512]{2,1,0:T(8,128)(2,1)S(1)}, u32[]{:S(2)}, u32[]{:S(2)}) collective-permute-start(bf16[4,128,512]{2,1,0:T(8,128)(2,1)S(1)} %pad_maximum_fusion.3.mine), channel_id=1, source_target_pairs={{0,1},{1,0},{2,3},{3,2},{4,5},{5,4},{6,7},{7,6},{8,9},{9,8},{10,11... | collective-permute-start | bytes 1572872 | tf_op jit(solution)/shard_map/ppermute | solution.py:247
  59.6 16.1 %collective-permute-start.19 = (bf16[128,2048]{1,0:T(8,128)(2,1)S(1)}, bf16[128,2048]{1,0:T(8,128)(2,1)S(1)}, u32[]{:S(2)}, u32[]{:S(2)}) collective-permute-start(bf16[128,2048]{1,0:T(8,128)(2,1)S(1)} %shard_map.58), channel_id=1, source_target_pairs={{0,8},{8,16},{16,24},{24,0},{1,9},{9,17},{17,25},{25,1},{2,10},{10... | collective-permute-start | bytes 1572872 | tf_op jit(solution)/shard_map/ppermute | solution.py:259

commit v2 on v1

--- a/solution.py
+++ b/solution.py
@@ -166,25 +166,34 @@
         pl.when(chip == n - 1)(functools.partial(body, n))
 
 
-def attend_planar(mask, live, queries, first, heads, group, mine, theirs):
+def attend_planar(mask, live, queries, q_first, group, kvs, kv_first, heads):
     rows = queries.shape[0]
     step = group * HEAD_SIZE
     smem = pl.BlockSpec(memory_space=pltpu.SMEM)
-    kv = pl.BlockSpec(mine.shape[:2] + (2 * HEAD_SIZE,), lambda h: (0, 0, h))
+    mine, theirs = kvs
+    kv = pl.BlockSpec(mine.shape[:2] + (2 * HEAD_SIZE,), lambda i: (0, 0, kv_first + i))
     return pl.pallas_call(
         functools.partial(planar_kernel, HEAD_SIZE**-0.5 * 1.4426950408889634),
         grid=(heads,),
         out_shape=jax.ShapeDtypeStruct((rows, heads * step), jnp.bfloat16),
-        in_specs=[smem, smem, pl.BlockSpec((rows, step), lambda h: (0, first + h)), kv, kv],
-        out_specs=pl.BlockSpec((rows, step), lambda h: (0, h)),
+        in_specs=[smem, smem, pl.BlockSpec((rows, step), lambda i: (0, q_first + i)), kv, kv],
+        out_specs=pl.BlockSpec((rows, step), lambda i: (0, i)),
         compiler_params=pltpu.CompilerParams(vmem_limit_bytes=40 * 2**20),
         cost_estimate=COST,
     )(mask, live, queries, mine, theirs)
 
 
-def pack_kernel(mask, live, q_ref, k_ref, v_ref, sent, *o_refs):
-    sent[:, : q_ref.shape[1]] = q_ref[...]
-    sent[:, sent.shape[1] - HEAD_SIZE :] = jnp.zeros_like(sent[:, :HEAD_SIZE])
+def pack_heads(k_ref, v_ref, first, ref, count):
+    for i in range(count):
+        cols = slice((first + i) * HEAD_SIZE, (first + i + 1) * HEAD_SIZE)
+        ref[:, 2 * i * HEAD_SIZE : (2 * i + 1) * HEAD_SIZE] = k_ref[:, cols]
+        ref[:, (2 * i + 1) * HEAD_SIZE : (2 * i + 2) * HEAD_SIZE] = v_ref[:, cols]
+
+
+def ahead_kernel(heads, mask, live, k_ref, v_ref, sent):
+    pack_heads(k_ref, v_ref, 0, sent, heads)
+    last = sent.shape[1] - HEAD_SIZE
+    sent[:, last:] = jnp.zeros_like(sent[:, last:])
     blocks = live.shape[0]
     deep = 16
     row = lax.broadcasted_iota(jnp.int32, (deep, HEAD_SIZE), 0)
@@ -194,37 +203,45 @@
         tile = jnp.where((row == blocks) & (col == j), live[j], tile)
         for i in range(blocks):
             tile = jnp.where((row == i) & (col == j), mask[i, j], tile)
-    sent[:deep, sent.shape[1] - HEAD_SIZE :] = tile.astype(jnp.float32).astype(sent.dtype)
-    head = 0
-    for n, ref in enumerate((sent,) + o_refs):
-        begin = 0 if n else q_ref.shape[1]
-        end = ref.shape[1] if n else ref.shape[1] - HEAD_SIZE
-        for at in range(begin, end, 2 * HEAD_SIZE):
-            cols = slice(head * HEAD_SIZE, (head + 1) * HEAD_SIZE)
-            ref[:, at : at + HEAD_SIZE] = k_ref[:, cols]
-            ref[:, at + HEAD_SIZE : at + 2 * HEAD_SIZE] = v_ref[:, cols]
-            head += 1
-
-
-def pack(mask, live, queries, keys, values, heads):
+    sent[:deep, last:] = tile.astype(jnp.float32).astype(sent.dtype)
+
+
+def whole(shape):
+    return pl.BlockSpec(shape, lambda i: (0, 0))
+
+
+def pack_ahead(mask, live, keys, values, heads):
+    rows = keys.shape[0]
+    smem = pl.BlockSpec(memory_space=pltpu.SMEM)
+    shape = (rows, heads * 2 * HEAD_SIZE + HEAD_SIZE)
+    kv = whole((rows, heads * HEAD_SIZE))
+    return pl.pallas_call(
+        functools.partial(ahead_kernel, heads),
+        grid=(1,),
+        out_shape=jax.ShapeDtypeStruct(shape, keys.dtype),
+        in_specs=[smem, smem, kv, kv],
+        out_specs=whole(shape),
+        cost_estimate=COST,
+    )(mask, live, keys, values)
+
+
+def rest_kernel(k_ref, v_ref, q_ref, sent, part, q_sent):
+    pack_heads(k_ref, v_ref, 0, part, part.shape[1] // (2 * HEAD_SIZE))
+    q_sent[...] = q_ref[...]
+
+
+def pack_rest(keys, values, queries, q_cols, sent):
     rows, cols = keys.shape
-    width = heads * 2 * HEAD_SIZE
-    count = cols // (heads * HEAD_SIZE) - 1
-    q_cols = heads * HEAD_SIZE * queries.shape[1] // cols
-    smem = pl.BlockSpec(memory_space=pltpu.SMEM)
-
-    def whole(shape):
-        return pl.BlockSpec(shape, lambda i: (0, 0))
-
-    shapes = [(rows, q_cols + width + HEAD_SIZE)] + [(rows, width)] * count
+    shapes = [(rows, cols), (rows, q_cols)]
+    later = pl.BlockSpec((rows, cols // 2), lambda i: (0, 1))
     return pl.pallas_call(
-        pack_kernel,
+        rest_kernel,
         grid=(1,),
         out_shape=[jax.ShapeDtypeStruct(shape, keys.dtype) for shape in shapes],
-        in_specs=[smem, smem, whole((rows, q_cols)), whole(keys.shape), whole(values.shape)],
+        in_specs=[later, later, whole((rows, q_cols)), pl.BlockSpec(memory_space=pl.ANY)],
         out_specs=[whole(shape) for shape in shapes],
         cost_estimate=COST,
-    )(mask, live, queries, keys, values)
+    )(keys, values, queries, sent)
 
 
 def pack_pairs(keys, values, heads):
@@ -236,7 +253,7 @@
 
 
 def after(value, *others):
-    return lax.optimization_barrier((value,) + others)[0]
+    return lax.optimization_barrier((value,) + others)[0] if others else value
 
 
 def on_plane(nsec, to):
@@ -258,35 +275,45 @@
     def on(value):
         return lax.ppermute(value, "section", onward)
 
-    sent, *parts = pack(mask, live, q, k, v, 2)
-    got = on(sent)
-
-    def gather(part):
-        return jnp.stack([part] + [exchange(part, nsec, by) for by in (2, 4, 6)])
-
-    def both_cores(mine):
-        return mine, exchange(mine, nsec, 1)
-
-    def run(mask, live, q, first, kvs):
-        return attend_planar(mask, live, q, first, 2, group, *kvs)
-
-    mine1 = gather(parts[0])
-    part2 = after(parts[1], mine1)
-    ctx1 = run(mask, live, q, 2, both_cores(mine1))
-    out1 = on(ctx1)
-    mine2 = after(gather(part2), ctx1, got)
-    part3 = after(parts[2], mine2)
-    ctx2 = run(mask, live, q, 4, both_cores(mine2))
-    out2 = on(ctx2)
-    mine3 = after(gather(part3), ctx2, out1)
-    part0 = after(got[:, 2 * step : -HEAD_SIZE], mine3)
-    ctx3 = run(mask, live, q, 6, both_cores(mine3))
-    out3 = on(ctx3)
-    kvs0 = both_cores(after(gather(part0), ctx3, out2))
+    half = keys.shape[2] // HEAD_SIZE // 2
+    sent = pack_ahead(mask, live, k, v, half)
+    part1, q01 = pack_rest(k, v, q, 2 * step, sent)
+    sent_in, q01_in = on(sent), on(q01)
+    q23_in = on(q[:, 2 * step : 4 * step])
+
+    def gather(part, *before):
+        near = [exchange(part, nsec, by) for by in (2, 4)]
+        return [part] + near + [exchange(after(part, *before), nsec, 6)]
+
+    def split(pieces, count):
+        width = pieces[0].shape[1] // count
+        return [jnp.stack([p[:, i * width : (i + 1) * width] for p in pieces]) for i in range(count)]
+
+    def swapped(mines):
+        if len(mines) == 1:
+            return mines[0], exchange(mines[0], nsec, 1)
+        return jnp.concatenate(mines, axis=2), jnp.concatenate([exchange(m, nsec, 1) for m in mines], axis=2)
+
+    mines1 = split(gather(part1, sent_in), 4)
+    mines1 = lax.optimization_barrier((*mines1, q01_in))[:4]
+    kvs1 = swapped(mines1)
+    ctx = attend_planar(mask, live, q, half, group, kvs1, 0, half)
+    out = on(ctx)
+    part0 = after(sent_in[:, :-HEAD_SIZE], mines1[0])
+    pieces0 = gather(part0, ctx)
     blocks = live.shape[0]
-    tab = got[: blocks + 1, -HEAD_SIZE:][:, :blocks].astype(jnp.int32)
-    first = run(tab[:-1], tab[-1], got, 0, kvs0)
-    return jnp.concatenate([first, out1, out2, out3], axis=1)[None]
+    tab = sent_in[: blocks + 1, -HEAD_SIZE:][:, :blocks].astype(jnp.int32)
+    mask_in, live_in = tab[:-1], tab[-1]
+    mines0 = split(pieces0, 4)
+    mines0 = lax.optimization_barrier((*mines0, q23_in, ctx))[:4]
+    theirs0 = [exchange(m, nsec, 1) for m in mines0]
+    heads = half // 4
+    ins = []
+    for i, kvs in enumerate(zip(mines0, theirs0)):
+        at = i * heads
+        q_in = q01_in if at < 2 else q23_in
+        ins.append(attend_planar(mask_in, live_in, q_in, at % 2, group, kvs, 0, heads))
+    return jnp.concatenate(ins + [out], axis=1)[None]
 
 
 def per_device(queries, keys, values, block_mask, block_live):

time: 77.4 us -> 66.1 us (0.85)
  waiting for transfers between devices: 41.6 us -> 27.9 us
  other arithmetic: 3.54 us -> 0.55 us
  local copies, waits for them, and re-layouts: 0.03 us -> 2.62 us
  Pallas kernels: 10.9 us -> 13 us
    ppermute x16 -> x14, waiting for transfers between devices: 25.3 us -> 11.3 us  [exchange(): lax.ppermute(part, ('section', 'seq'), on_plane(nsec, lambda i: i ^ by))]
    ppermute x4, starting transfers between devices: 4.01 us -> 5.85 us  [on(): return lax.ppermute(value, 'section', onward)]
    another operation x4 -> x6, other arithmetic: 2.08 us -> 0.29 us  [split(): jnp.stack([p[:, i * width:(i + 1) * width] for p in pieces])]
    pallas_call x1 -> x2, Pallas kernels: 2.45 us -> 3.93 us  [the longest x1 2.13 us: pack_rest(): pl.pallas_call(rest_kernel, grid=(1,), out_shape=[jax.ShapeDtypeStruct(sh...]
    broadcast_in_dim x1 -> x0, other arithmetic: 1.46 us -> none  [per_device_8(): return jnp.concatenate([first, out1, out2, out3], axis=1)[None]]
    unnamed x8 -> x12, local copies, waits for them, and re-layouts: 0.02 us -> 1.41 us
    ppermute x16 -> x14, starting transfers between devices: 17 us -> 15.7 us  [exchange(): lax.ppermute(part, ('section', 'seq'), on_plane(nsec, lambda i: i ^ by))]
    another operation x0 -> x8, local copies, waits for them, and re-layouts: none -> 1.09 us  [split(): jnp.stack([p[:, i * width:(i + 1) * width] for p in pieces])]
  transfers between devices with their start and end apart: 20 -> 18, of which waited for: 15 -> 7; matrix products, arithmetic and copies ran while one was open for 3% -> 3% of each run, Pallas kernels for 11% -> 17%
where the time goes in v2:
time: 66.1 us; the launch traced here: 65.9 us
  waiting for transfers between devices  27.9 us (42%)
  starting transfers between devices  21.5 us (33%)
  Pallas kernels  13 us (20%)
  local copies, waits for them, and re-layouts  2.62 us (4%)
    ppermute x4, waiting for transfers between devices, on(): return lax.ppermute(value, 'section', onward)  16.6 us
    ppermute x14, starting transfers between devices, exchange(): lax.ppermute(part, ('section', 'seq'), on_plane(nsec, lambda i: i ^ by))  15.7 us
    ppermute x14, waiting for transfers between devices, exchange(): lax.ppermute(part, ('section', 'seq'), on_plane(nsec, lambda i: i ^ by))  11.3 us
    pallas_call x5, Pallas kernels, attend_planar(): pl.pallas_call(functools.partial(planar_kernel, HEAD_SIZE ** (-0.5) * 1.4...  9.06 us
    ppermute x4, starting transfers between devices, on(): return lax.ppermute(value, 'section', onward)  5.85 us
    pallas_call x1, Pallas kernels, pack_rest(): pl.pallas_call(rest_kernel, grid=(1,), out_shape=[jax.ShapeDtypeStruct(sh...  2.13 us
    pallas_call x1, Pallas kernels, pack_ahead(): pl.pallas_call(functools.partial(ahead_kernel, heads), grid=(1,), out_sha...  1.8 us
    unnamed x12, local copies, waits for them, and re-layouts  1.41 us
  transfers between devices with their start and end apart: 18, of which 7 were waited for; matrix products, arithmetic and copies ran while one was open for 3% of the time, Pallas kernels for 17%

profile of v2, /device:TPU:0, one launch (start us, length us, event | category | flops | bytes accessed | tf_op | source)
XLA Modules:
  0.0 65.9 jit_solution(12494723698997187126)
XLA Ops:
  0.0 1.8 %shard_map.55.sent = bf16[128,1152]{1,0:T(8,128)(2,1)} custom-call(s32[8,8]{1,0:T(8,128)} %bitcast.75, s32[8]{0:T(128)} %bitcast.77, bf16[128,1024]{1,0:T(8,128)(2,1)} %bitcast.79, bf16[128,1024]{1,0:T(8,128)(2,1)} %bitcast.81), custom_call_target="tpu_custom_call" | custom-call | flops 1 | bytes 1 | tf_op jit(solution)/shard_map/pallas_call | solution.py:218
  1.8 3.0 %collective-permute-start = (bf16[128,1152]{1,0:T(8,128)(2,1)}, bf16[128,1152]{1,0:T(8,128)(2,1)S(1)}, u32[]{:S(2)}, u32[]{:S(2)}) collective-permute-start(bf16[128,1152]{1,0:T(8,128)(2,1)} %shard_map.55.sent), channel_id=1, source_target_pairs={{0,8},{8,16},{16,24},{24,0},{1,9},{9,17},{17,25},{25,1},{2,10},{10... | collective-permute-start | bytes 884744 | tf_op jit(solution)/shard_map/ppermute | solution.py:276
  4.8 2.1 %shard_map.56 = (bf16[128,1024]{1,0:T(8,128)(2,1)}, bf16[128,2048]{1,0:T(8,128)(2,1)}) custom-call(bf16[128,1024]{1,0:T(8,128)(2,1)} %bitcast.80, bf16[128,1024]{1,0:T(8,128)(2,1)} %bitcast.82, bf16[128,8192]{1,0:T(8,128)(2,1)} %bitcast.72, bf16[128,1152]{1,0:T(8,128)(2,1)} %shard_map.55.sent), custom_call_target="tpu_custom_call" | custom-call | flops 1 | bytes 1 | tf_op jit(solution)/shard_map/pallas_call | solution.py:237
  7.0 1.5 %collective-permute-start.3 = (bf16[128,1024]{1,0:T(8,128)(2,1)}, bf16[128,1024]{1,0:T(8,128)(2,1)S(1)}, u32[]{:S(2)}, u32[]{:S(2)}) collective-permute-start(bf16[128,1024]{1,0:T(8,128)(2,1)} %get-tuple-element.20), channel_id=1, source_target_pairs={{0,4},{1,5},{2,6},{3,7},{4,0},{5,1},{6,2},{7,3},{8,12},{9,13},{10,... | collective-permute-start | bytes 786440 | tf_op jit(solution)/shard_map/ppermute | solution.py:264
  8.5 1.5 %collective-permute-start.2 = (bf16[128,1024]{1,0:T(8,128)(2,1)}, bf16[128,1024]{1,0:T(8,128)(2,1)S(1)}, u32[]{:S(2)}, u32[]{:S(2)}) collective-permute-start(bf16[128,1024]{1,0:T(8,128)(2,1)} %get-tuple-element.20), channel_id=1, source_target_pairs={{0,2},{1,3},{2,0},{3,1},{4,6},{5,7},{6,4},{7,5},{8,10},{9,11},{10,... | collective-permute-start | bytes 786440 | tf_op jit(solution)/shard_map/ppermute | solution.py:264
  10.0 1.6 %collective-permute-start.1 = (bf16[128,2048]{1,0:T(8,128)(2,1)}, bf16[128,2048]{1,0:T(8,128)(2,1)S(1)}, u32[]{:S(2)}, u32[]{:S(2)}) collective-permute-start(bf16[128,2048]{1,0:T(8,128)(2,1)} %get-tuple-element.18), channel_id=1, source_target_pairs={{0,8},{8,16},{16,24},{24,0},{1,9},{9,17},{17,25},{25,1},{2,10},{10... | collective-permute-start | bytes 1572872 | tf_op jit(solution)/shard_map/ppermute | solution.py:276
  11.5 1.0 %slice_bitcast_fusion.28 = (bf16[1,128,256]{2,1,0:T(8,128)(2,1)S(1)}, bf16[1,128,256]{2,1,0:T(8,128)(2,1)S(1)}, bf16[1,128,256]{2,1,0:T(8,128)(2,1)S(1)}, bf16[1,128,256]{2,1,0:T(8,128)(2,1)S(1)}) fusion(bf16[128,1024]{1,0:T(8,128)(2,1)} %get-tuple-element.20), kind=kLoop, calls=%fused_computation.38 | loop fusion | bytes 524288 | tf_op jit(solution)/shard_map/stack | solution.py:290
  12.5 2.0 %collective-permute-done = bf16[128,1152]{1,0:T(8,128)(2,1)S(1)} collective-permute-done((bf16[128,1152]{1,0:T(8,128)(2,1)}, bf16[128,1152]{1,0:T(8,128)(2,1)S(1)}, u32[]{:S(2)}, u32[]{:S(2)}) %collective-permute-start) | collective-permute-done | bytes 294944 | tf_op jit(solution)/shard_map/ppermute | solution.py:276
  14.5 3.1 %collective-permute-start.4 = (bf16[128,1024]{1,0:T(8,128)(2,1)}, bf16[128,1024]{1,0:T(8,128)(2,1)S(1)}, u32[]{:S(2)}, u32[]{:S(2)}) collective-permute-start(bf16[128,1024]{1,0:T(8,128)(2,1)} %get-tuple-element.20), channel_id=1, source_target_pairs={{0,6},{1,7},{2,4},{3,5},{4,2},{5,3},{6,0},{7,1},{8,14},{9,15},{10,... | collective-permute-start | bytes 786440 | tf_op jit(solution)/shard_map/ppermute | solution.py:264
  17.7 5.0 %collective-permute-done.4 = bf16[128,1024]{1,0:T(8,128)(2,1)S(1)} collective-permute-done((bf16[128,1024]{1,0:T(8,128)(2,1)}, bf16[128,1024]{1,0:T(8,128)(2,1)S(1)}, u32[]{:S(2)}, u32[]{:S(2)}) %collective-permute-start.4) | collective-permute-done | bytes 262176 | tf_op jit(solution)/shard_map/ppermute | solution.py:264
  22.9 2.5 %collective-permute-done.1.q_ref = bf16[128,2048]{1,0:T(8,128)(2,1)S(1)} collective-permute-done((bf16[128,2048]{1,0:T(8,128)(2,1)}, bf16[128,2048]{1,0:T(8,128)(2,1)S(1)}, u32[]{:S(2)}, u32[]{:S(2)}) %collective-permute-start.1) | collective-permute-done | bytes 524320 | tf_op jit(solution)/shard_map/ppermute | solution.py:276
  25.3 0.5 collective-permute-start.9
  25.8 0.5 collective-permute-start.7
  26.5 0.1 pad_maximum_fusion.mine
  26.6 0.2 collective-permute-done.8
  26.8 1.5 %collective-permute-start.6 = (bf16[128,1024]{1,0:T(8,128)(2,1)S(1)}, bf16[128,1024]{1,0:T(8,128)(2,1)S(1)}, u32[]{:S(2)}, u32[]{:S(2)}) collective-permute-start(bf16[128,1024]{1,0:T(8,128)(2,1)S(1)} %slice.153), channel_id=1, source_target_pairs={{0,4},{1,5},{2,6},{3,7},{4,0},{5,1},{6,2},{7,3},{8,12},{9,13},{10,... | collective-permute-start | bytes 786440 | tf_op jit(solution)/shard_map/ppermute | solution.py:264
  28.4 1.5 %collective-permute-start.5 = (bf16[128,1024]{1,0:T(8,128)(2,1)S(1)}, bf16[128,1024]{1,0:T(8,128)(2,1)S(1)}, u32[]{:S(2)}, u32[]{:S(2)}) collective-permute-start(bf16[128,1024]{1,0:T(8,128)(2,1)S(1)} %slice.153), channel_id=1, source_target_pairs={{0,2},{1,3},{2,0},{3,1},{4,6},{5,7},{6,4},{7,5},{8,10},{9,11},{10,... | collective-permute-start | bytes 786440 | tf_op jit(solution)/shard_map/ppermute | solution.py:264
  29.9 0.1 pad_maximum_fusion.1.theirs
  30.0 3.8 %shard_map.57 = bf16[128,4096]{1,0:T(8,128)(2,1)S(1)} custom-call(s32[8,8]{1,0:T(8,128)S(1)} %bitcast.76, s32[8]{0:T(128)S(1)} %bitcast.78, bf16[128,8192]{1,0:T(8,128)(2,1)S(1)} %bitcast.74, bf16[4,128,1024]{2,1,0:T(8,128)(2,1)S(1)} %pad_maximum_fusion.mine, bf16[4,128,1024]{2,1,0:T(8,128)(2,1)S(1)} %pad_maximum_fusion.1.theirs), custom_call_target="tpu_custom_call" | custom-call | flops 1 | bytes 1 | tf_op jit(solution)/shard_map/pallas_call | solution.py:175
  33.8 1.2 %collective-permute-start.17 = (bf16[128,4096]{1,0:T(8,128)(2,1)S(1)}, bf16[128,4096]{1,0:T(8,128)(2,1)S(1)}, u32[]{:S(2)}, u32[]{:S(2)}) collective-permute-start(bf16[128,4096]{1,0:T(8,128)(2,1)S(1)} %shard_map.57), channel_id=1, source_target_pairs={{0,8},{8,16},{16,24},{24,0},{1,9},{9,17},{17,25},{25,1},{2,10},{10... | collective-permute-start | bytes 3145736 | tf_op jit(solution)/shard_map/ppermute | solution.py:276
  35.0 4.5 %collective-permute-start.11 = (bf16[128,1024]{1,0:T(8,128)(2,1)S(1)}, bf16[128,1024]{1,0:T(8,128)(2,1)S(1)}, u32[]{:S(2)}, u32[]{:S(2)}) collective-permute-start(bf16[128,1024]{1,0:T(8,128)(2,1)S(1)} %slice.153), channel_id=1, source_target_pairs={{0,6},{1,7},{2,4},{3,5},{4,2},{5,3},{6,0},{7,1},{8,14},{9,15},{10,... | collective-permute-start | bytes 786440 | tf_op jit(solution)/shard_map/ppermute | solution.py:264
  39.6 5.6 %collective-permute-done.11 = bf16[128,1024]{1,0:T(8,128)(2,1)S(1)} collective-permute-done((bf16[128,1024]{1,0:T(8,128)(2,1)S(1)}, bf16[128,1024]{1,0:T(8,128)(2,1)S(1)}, u32[]{:S(2)}, u32[]{:S(2)}) %collective-permute-start.11) | collective-permute-done | bytes 262176 | tf_op jit(solution)/shard_map/ppermute | solution.py:264
  45.4 0.5 collective-permute-start.14
  45.9 0.1 collective-permute-start.15
  46.0 0.4 collective-permute-start.16
  46.4 0.5 collective-permute-done.13.theirs
  46.9 1.3 %shard_map.58 = bf16[128,1024]{1,0:T(8,128)(2,1)S(1)} custom-call(s32[8,8]{1,0:T(8,128)S(1)} %slice.151.mask, s32[8]{0:T(128)S(1)} %slice_bitcast_fusion.32.live, bf16[128,2048]{1,0:T(8,128)(2,1)S(1)} %collective-permute-done.1.q_ref, bf16[4,128,256]{2,1,0:T(8,128)(2,1)S(1)} %pad_maximum_fusion.6.mine, bf16[4,128,256]{2,1,0:T(8,128)(2,1)S(1)} %collective-permute-done.13.theirs), custom_call_target="tpu_custom_call" | custom-call | flops 1 | bytes 1 | tf_op jit(solution)/shard_map/pallas_call | solution.py:175
  48.2 1.5 %shard_map.59 = bf16[128,1024]{1,0:T(8,128)(2,1)S(1)} custom-call(s32[8,8]{1,0:T(8,128)S(1)} %slice.151.mask, s32[8]{0:T(128)S(1)} %slice_bitcast_fusion.32.live, bf16[128,2048]{1,0:T(8,128)(2,1)S(1)} %collective-permute-done.1.q_ref, bf16[4,128,256]{2,1,0:T(8,128)(2,1)S(1)} %pad_maximum_fusion.7.mine, bf16[4,128,256]{2,1,0:T(8,128)(2,1)S(1)} %collective-permute-done.14.theirs), custom_call_target="tpu_custom_call" | custom-call | flops 1 | bytes 1 | tf_op jit(solution)/shard_map/pallas_call | solution.py:175
  49.7 1.3 %shard_map.60 = bf16[128,1024]{1,0:T(8,128)(2,1)S(1)} custom-call(s32[8,8]{1,0:T(8,128)S(1)} %slice.151.mask, s32[8]{0:T(128)S(1)} %slice_bitcast_fusion.32.live, bf16[128,2048]{1,0:T(8,128)(2,1)S(1)} %collective-permute-done.12.q_ref, bf16[4,128,256]{2,1,0:T(8,128)(2,1)S(1)} %pad_maximum_fusion.8.mine, bf16[4,128,256]{2,1,0:T(8,128)(2,1)S(1)} %collective-permute-done.15.theirs), custom_call_target="tpu_custom_call" | custom-call | flops 1 | bytes 1 | tf_op jit(solution)/shard_map/pallas_call | solution.py:175
  51.0 1.3 %shard_map.61 = bf16[128,1024]{1,0:T(8,128)(2,1)S(1)} custom-call(s32[8,8]{1,0:T(8,128)S(1)} %slice.151.mask, s32[8]{0:T(128)S(1)} %slice_bitcast_fusion.32.live, bf16[128,2048]{1,0:T(8,128)(2,1)S(1)} %collective-permute-done.12.q_ref, bf16[4,128,256]{2,1,0:T(8,128)(2,1)S(1)} %pad_maximum_fusion.9.mine, bf16[4,128,256]{2,1,0:T(8,128)(2,1)S(1)} %collective-permute-done.16.theirs), custom_call_target="tpu_custom_call" | custom-call | flops 1 | bytes 1 | tf_op jit(solution)/shard_map/pallas_call | solution.py:175
  52.4 12.2 %collective-permute-done.17 = bf16[128,4096]{1,0:T(8,128)(2,1)S(1)} collective-permute-done((bf16[128,4096]{1,0:T(8,128)(2,1)S(1)}, bf16[128,4096]{1,0:T(8,128)(2,1)S(1)}, u32[]{:S(2)}, u32[]{:S(2)}) %collective-permute-start.17) | collective-permute-done | bytes 1048608 | tf_op jit(solution)/shard_map/ppermute | solution.py:276
  64.6 1.3 %copy-done.3 = bf16[128,8192]{1,0:T(8,128)(2,1)} copy-done((bf16[128,8192]{1,0:T(8,128)(2,1)}, bf16[128,8192]{1,0:T(8,128)(2,1)S(1)}, u32[]{:S(2)}) %copy-start.3) | copy-done | bytes 2097176
  (45 shorter events, 0.8 us)
Async XLA Ops:
  1.8 12.7 %collective-permute-start = (bf16[128,1152]{1,0:T(8,128)(2,1)}, bf16[128,1152]{1,0:T(8,128)(2,1)S(1)}, u32[]{:S(2)}, u32[]{:S(2)}) collective-permute-start(bf16[128,1152]{1,0:T(8,128)(2,1)} %shard_map.55.sent), channel_id=1, source_target_pairs={{0,8},{8,16},{16,24},{24,0},{1,9},{9,17},{17,25},{25,1},{2,10},{10... | collective-permute-start | bytes 884744 | tf_op jit(solution)/shard_map/ppermute | solution.py:276
  7.0 10.6 %collective-permute-start.3 = (bf16[128,1024]{1,0:T(8,128)(2,1)}, bf16[128,1024]{1,0:T(8,128)(2,1)S(1)}, u32[]{:S(2)}, u32[]{:S(2)}) collective-permute-start(bf16[128,1024]{1,0:T(8,128)(2,1)} %get-tuple-element.20), channel_id=1, source_target_pairs={{0,4},{1,5},{2,6},{3,7},{4,0},{5,1},{6,2},{7,3},{8,12},{9,13},{10,... | collective-permute-start | bytes 786440 | tf_op jit(solution)/shard_map/ppermute | solution.py:264
  8.5 9.1 %collective-permute-start.2 = (bf16[128,1024]{1,0:T(8,128)(2,1)}, bf16[128,1024]{1,0:T(8,128)(2,1)S(1)}, u32[]{:S(2)}, u32[]{:S(2)}) collective-permute-start(bf16[128,1024]{1,0:T(8,128)(2,1)} %get-tuple-element.20), channel_id=1, source_target_pairs={{0,2},{1,3},{2,0},{3,1},{4,6},{5,7},{6,4},{7,5},{8,10},{9,11},{10,... | collective-permute-start | bytes 786440 | tf_op jit(solution)/shard_map/ppermute | solution.py:264
  10.0 16.4 %copy-start = (bf16[1,128,8192]{2,1,0:T(8,128)(2,1)S(1)}, bf16[1,128,8192]{2,1,0:T(8,128)(2,1)}, u32[]{:S(2)}) copy-start(bf16[1,128,8192]{2,1,0:T(8,128)(2,1)} %param.5) | copy-start | bytes 6291460
  10.0 15.3 %collective-permute-start.1 = (bf16[128,2048]{1,0:T(8,128)(2,1)}, bf16[128,2048]{1,0:T(8,128)(2,1)S(1)}, u32[]{:S(2)}, u32[]{:S(2)}) collective-permute-start(bf16[128,2048]{1,0:T(8,128)(2,1)} %get-tuple-element.18), channel_id=1, source_target_pairs={{0,8},{8,16},{16,24},{24,0},{1,9},{9,17},{17,25},{25,1},{2,10},{10... | collective-permute-start | bytes 1572872 | tf_op jit(solution)/shard_map/ppermute | solution.py:276
  14.5 8.2 %collective-permute-start.4 = (bf16[128,1024]{1,0:T(8,128)(2,1)}, bf16[128,1024]{1,0:T(8,128)(2,1)S(1)}, u32[]{:S(2)}, u32[]{:S(2)}) collective-permute-start(bf16[128,1024]{1,0:T(8,128)(2,1)} %get-tuple-element.20), channel_id=1, source_target_pairs={{0,6},{1,7},{2,4},{3,5},{4,2},{5,3},{6,0},{7,1},{8,14},{9,15},{10,... | collective-permute-start | bytes 786440 | tf_op jit(solution)/shard_map/ppermute | solution.py:264
  25.3 1.5 %collective-permute-start.8 = (bf16[4,128,256]{2,1,0:T(8,128)(2,1)S(1)}, bf16[4,128,256]{2,1,0:T(8,128)(2,1)S(1)}, u32[]{:S(2)}, u32[]{:S(2)}) collective-permute-start(bf16[4,128,256]{2,1,0:T(8,128)(2,1)S(1)} %get-tuple-element.23), channel_id=1, source_target_pairs={{0,1},{1,0},{2,3},{3,2},{4,5},{5,4},{6,7},{7,6},{8,9},{9,8},{10,11... | collective-permute-start | bytes 786440 | tf_op jit(solution)/shard_map/ppermute | solution.py:264
  25.3 3.1 %collective-permute-start.9 = (bf16[4,128,256]{2,1,0:T(8,128)(2,1)S(1)}, bf16[4,128,256]{2,1,0:T(8,128)(2,1)S(1)}, u32[]{:S(2)}, u32[]{:S(2)}) collective-permute-start(bf16[4,128,256]{2,1,0:T(8,128)(2,1)S(1)} %get-tuple-element.24), channel_id=1, source_target_pairs={{0,1},{1,0},{2,3},{3,2},{4,5},{5,4},{6,7},{7,6},{8,9},{9,8},{10,11... | collective-permute-start | bytes 786440 | tf_op jit(solution)/shard_map/ppermute | solution.py:264
  25.8 4.0 %collective-permute-start.10 = (bf16[4,128,256]{2,1,0:T(8,128)(2,1)S(1)}, bf16[4,128,256]{2,1,0:T(8,128)(2,1)S(1)}, u32[]{:S(2)}, u32[]{:S(2)}) collective-permute-start(bf16[4,128,256]{2,1,0:T(8,128)(2,1)S(1)} %get-tuple-element.25), channel_id=1, source_target_pairs={{0,1},{1,0},{2,3},{3,2},{4,5},{5,4},{6,7},{7,6},{8,9},{9,8},{10,11... | collective-permute-start | bytes 786440 | tf_op jit(solution)/shard_map/ppermute | solution.py:264
  25.8 4.0 %collective-permute-start.7 = (bf16[4,128,256]{2,1,0:T(8,128)(2,1)S(1)}, bf16[4,128,256]{2,1,0:T(8,128)(2,1)S(1)}, u32[]{:S(2)}, u32[]{:S(2)}) collective-permute-start(bf16[4,128,256]{2,1,0:T(8,128)(2,1)S(1)} %get-tuple-element.21), channel_id=1, source_target_pairs={{0,1},{1,0},{2,3},{3,2},{4,5},{5,4},{6,7},{7,6},{8,9},{9,8},{10,11... | collective-permute-start | bytes 786440 | tf_op jit(solution)/shard_map/ppermute | solution.py:264
  26.4 18.9 %collective-permute-start.12 = (bf16[128,2048]{1,0:T(8,128)(2,1)S(1)}, bf16[128,2048]{1,0:T(8,128)(2,1)S(1)}, u32[]{:S(2)}, u32[]{:S(2)}) collective-permute-start(bf16[128,2048]{1,0:T(8,128)(2,1)S(1)} %slice.178), channel_id=1, source_target_pairs={{0,8},{8,16},{16,24},{24,0},{1,9},{9,17},{17,25},{25,1},{2,10},{10... | collective-permute-start | bytes 1572872 | tf_op jit(solution)/shard_map/ppermute | solution.py:276
  26.5 3.6 %copy-start.1 = (s32[1,8,8]{2,1,0:T(8,128)S(1)}, s32[1,8,8]{2,1,0:T(8,128)}, u32[]{:S(2)}) copy-start(s32[1,8,8]{2,1,0:T(8,128)} %param.8) | copy-start | bytes 772
  26.5 3.6 %copy-start.2 = (s32[1,8]{1,0:T(1,128)S(1)}, s32[1,8]{1,0:T(1,128)}, u32[]{:S(2)}) copy-start(s32[1,8]{1,0:T(1,128)} %param.9) | copy-start | bytes 100
  26.8 12.6 %collective-permute-start.6 = (bf16[128,1024]{1,0:T(8,128)(2,1)S(1)}, bf16[128,1024]{1,0:T(8,128)(2,1)S(1)}, u32[]{:S(2)}, u32[]{:S(2)}) collective-permute-start(bf16[128,1024]{1,0:T(8,128)(2,1)S(1)} %slice.153), channel_id=1, source_target_pairs={{0,4},{1,5},{2,6},{3,7},{4,0},{5,1},{6,2},{7,3},{8,12},{9,13},{10,... | collective-permute-start | bytes 786440 | tf_op jit(solution)/shard_map/ppermute | solution.py:264
  28.4 11.1 %collective-permute-start.5 = (bf16[128,1024]{1,0:T(8,128)(2,1)S(1)}, bf16[128,1024]{1,0:T(8,128)(2,1)S(1)}, u32[]{:S(2)}, u32[]{:S(2)}) collective-permute-start(bf16[128,1024]{1,0:T(8,128)(2,1)S(1)} %slice.153), channel_id=1, source_target_pairs={{0,2},{1,3},{2,0},{3,1},{4,6},{5,7},{6,4},{7,5},{8,10},{9,11},{10,... | collective-permute-start | bytes 786440 | tf_op jit(solution)/shard_map/ppermute | solution.py:264
  33.8 30.7 %collective-permute-start.17 = (bf16[128,4096]{1,0:T(8,128)(2,1)S(1)}, bf16[128,4096]{1,0:T(8,128)(2,1)S(1)}, u32[]{:S(2)}, u32[]{:S(2)}) collective-permute-start(bf16[128,4096]{1,0:T(8,128)(2,1)S(1)} %shard_map.57), channel_id=1, source_target_pairs={{0,8},{8,16},{16,24},{24,0},{1,9},{9,17},{17,25},{25,1},{2,10},{10... | collective-permute-start | bytes 3145736 | tf_op jit(solution)/shard_map/ppermute | solution.py:276
  35.0 10.1 %collective-permute-start.11 = (bf16[128,1024]{1,0:T(8,128)(2,1)S(1)}, bf16[128,1024]{1,0:T(8,128)(2,1)S(1)}, u32[]{:S(2)}, u32[]{:S(2)}) collective-permute-start(bf16[128,1024]{1,0:T(8,128)(2,1)S(1)} %slice.153), channel_id=1, source_target_pairs={{0,6},{1,7},{2,4},{3,5},{4,2},{5,3},{6,0},{7,1},{8,14},{9,15},{10,... | collective-permute-start | bytes 786440 | tf_op jit(solution)/shard_map/ppermute | solution.py:264
  45.3 1.6 %collective-permute-start.13 = (bf16[4,128,256]{2,1,0:T(8,128)(2,1)S(1)}, bf16[4,128,256]{2,1,0:T(8,128)(2,1)S(1)}, u32[]{:S(2)}, u32[]{:S(2)}) collective-permute-start(bf16[4,128,256]{2,1,0:T(8,128)(2,1)S(1)} %pad_maximum_fusion.6.mine), channel_id=1, source_target_pairs={{0,1},{1,0},{2,3},{3,2},{4,5},{5,4},{6,7},{7,6},{8,9},{9,8},{10,11... | collective-permute-start | bytes 786440 | tf_op jit(solution)/shard_map/ppermute | solution.py:264
  45.4 2.8 %collective-permute-start.14 = (bf16[4,128,256]{2,1,0:T(8,128)(2,1)S(1)}, bf16[4,128,256]{2,1,0:T(8,128)(2,1)S(1)}, u32[]{:S(2)}, u32[]{:S(2)}) collective-permute-start(bf16[4,128,256]{2,1,0:T(8,128)(2,1)S(1)} %pad_maximum_fusion.7.mine), channel_id=1, source_target_pairs={{0,1},{1,0},{2,3},{3,2},{4,5},{5,4},{6,7},{7,6},{8,9},{9,8},{10,11... | collective-permute-start | bytes 786440 | tf_op jit(solution)/shard_map/ppermute | solution.py:264
  45.9 3.8 %collective-permute-start.15 = (bf16[4,128,256]{2,1,0:T(8,128)(2,1)S(1)}, bf16[4,128,256]{2,1,0:T(8,128)(2,1)S(1)}, u32[]{:S(2)}, u32[]{:S(2)}) collective-permute-start(bf16[4,128,256]{2,1,0:T(8,128)(2,1)S(1)} %pad_maximum_fusion.8.mine), channel_id=1, source_target_pairs={{0,1},{1,0},{2,3},{3,2},{4,5},{5,4},{6,7},{7,6},{8,9},{9,8},{10,11... | collective-permute-start | bytes 786440 | tf_op jit(solution)/shard_map/ppermute | solution.py:264
  46.0 5.0 %collective-permute-start.16 = (bf16[4,128,256]{2,1,0:T(8,128)(2,1)S(1)}, bf16[4,128,256]{2,1,0:T(8,128)(2,1)S(1)}, u32[]{:S(2)}, u32[]{:S(2)}) collective-permute-start(bf16[4,128,256]{2,1,0:T(8,128)(2,1)S(1)} %pad_maximum_fusion.9.mine), channel_id=1, source_target_pairs={{0,1},{1,0},{2,3},{3,2},{4,5},{5,4},{6,7},{7,6},{8,9},{9,8},{10,11... | collective-permute-start | bytes 786440 | tf_op jit(solution)/shard_map/ppermute | solution.py:264
  64.6 1.3 %copy-start.3 = (bf16[128,8192]{1,0:T(8,128)(2,1)}, bf16[128,8192]{1,0:T(8,128)(2,1)S(1)}, u32[]{:S(2)}) copy-start(bf16[128,8192]{1,0:T(8,128)(2,1)S(1)} %constant_dynamic-update-slice_fusion) | copy-start | bytes 6291460
